TPU v7x, 128 devices: a whole 4x4x4 slice. The times are simulated.
128 devices in a mesh: member: 8 (over y, z_hi), space: 16 (over x, z_lo, core).
Axes of the slice: x: 4, y: 4, z: 4 (z_hi: 2, z_lo: 2; z = z_hi * 2 + z_lo), core: 2. Of those that a mesh axis runs over, the one named last changes fastest.
Arguments:
- latent: bfloat16 [16, 2048, 1024], P('member', 'space'), may hold values from -17 to 17
- predictions: float32 [16, 100, 2048], P('member', None, 'space'), may hold values from -6 to 6
- target: float32 [100, 2048], P(None, 'space'), may hold values from -6 to 6
- area_weight: float32 [2048], P('space'), may hold values from 0.1 to 1
- slab_count: int32 [16], P('space'), may hold values from 64 to 128, as said below
- w_qkv: bfloat16 [1024, 3072], replicated, may hold values from -4 to 4
- w_o: bfloat16 [1024, 1024], replicated, may hold values from -0.1875 to 0.1875
- w_out: bfloat16 [1024, 100], replicated, may hold values from -0.1875 to 0.1875
Outputs:
- grad_latent: bfloat16 [16, 2048, 1024], P('member', 'space')
- grad_qkv: float32 [1024, 3072], P(('member', 'space'))
- grad_o: float32 [1024, 1024], P(('member', 'space'))
- grad_out: float32 [1024, 100], P(('member', 'space'))
Inputs may be any that keep to these rules, and one draw needn't show every extreme that they name: `slab_count`: at least one slab has all 128 slots live.
All inputs are finite; a program needn't handle non-finite values.
Results may differ from a plain program's by a relative error of at most 0.03.
The roundings to bfloat16 on the way count: a program that leaves them out, or rounds other values in their place, can miss the bound.
Values may be sent and summed in bfloat16 or wider, within the bound.
A program may use at most 128 MiB of HBM per device.

v0:
```python
import jax
import jax.numpy as jnp
from jax import lax
from jax.sharding import PartitionSpec as P

HEAD_DIM = 64
BLOCK = 128


def extended(value, sides, width):
    for axis, dim in sides:
        count, length = (lax.axis_size(axis), value.shape[dim])
        up = [(i, (i + 1) % count) for i in range(count - 1)]
        down = [(j, i) for i, j in up]
        last = lax.slice_in_dim(value, length - width, length, axis=dim)
        leading = lax.slice_in_dim(value, 0, width, axis=dim)
        before = lax.ppermute(last, axis, up)
        after = lax.ppermute(leading, axis, down)
        value = jnp.concatenate([before, value, after], axis=dim)
    return value


def crps_terms(own, every, target_part, weight_part, total):
    first = jnp.sign(own - target_part[None])
    pair = jnp.sum(jnp.sign(own[:, None] - every[None]), axis=1)
    return weight_part[None, None, :] * (first - pair / (total - 1))


def on_device(latent, predictions, target, area_weight, slab_count, w_qkv, w_o, w_out):
    members_here, points, width = latent.shape
    place = jnp.arange(points)
    live = place < slab_count[0]
    pweight = jnp.where(live, area_weight, jnp.zeros_like(area_weight))
    total = lax.axis_size("member") * members_here
    every = lax.all_gather(predictions, "member", axis=0, tiled=True)
    crps = crps_terms(predictions, every, target, pweight, total)
    xf = latent.astype(jnp.float32)
    mean = jnp.mean(xf, axis=-1, keepdims=True)
    cent = xf - mean
    var = jnp.mean(cent * cent, axis=-1, keepdims=True)
    rstd = lax.rsqrt(var + 1e-05)
    norm = cent * rstd
    xn = norm.astype(jnp.bfloat16)
    qkv = jnp.einsum("mpd,de->mpe", xn, w_qkv, preferred_element_type=jnp.float32).astype(
        jnp.bfloat16
    )
    query = qkv[..., :width]
    keyval = qkv[..., width:]
    wide = extended(keyval, (("space", 1),), BLOCK)
    nblk = points // BLOCK
    heads = width // HEAD_DIM
    scale = HEAD_DIM ** (-0.5)
    blocks = wide.reshape(members_here, nblk + 2, BLOCK, 2 * width)
    window = jnp.concatenate([blocks[:, :-2], blocks[:, 1:-1], blocks[:, 2:]], axis=2)
    qh = query.reshape(members_here, nblk, BLOCK, heads, HEAD_DIM)
    kh = window[..., :width].reshape(members_here, nblk, 3 * BLOCK, heads, HEAD_DIM)
    vh = window[..., width:].reshape(members_here, nblk, 3 * BLOCK, heads, HEAD_DIM)
    slab = lax.axis_index("space")
    final = lax.axis_size("space") - 1
    ext = jnp.arange(nblk)[:, None] + (jnp.arange(3 * BLOCK) // BLOCK)[None, :]
    valid = ((ext >= 1) | (slab > 0)) & ((ext <= nblk) | (slab < final))
    scores = jnp.einsum("mnqhd,mnkhd->mnhqk", qh, kh, preferred_element_type=jnp.float32) * scale
    scores = jnp.where(valid[None, :, None, None, :], scores, -1e30)
    prob = jax.nn.softmax(scores, axis=-1)
    prob_b = prob.astype(jnp.bfloat16)
    attended = jnp.einsum("mnhqk,mnkhd->mnqhd", prob_b, vh, preferred_element_type=jnp.float32)
    attended = attended.astype(jnp.bfloat16).reshape(members_here, points, width)
    after = (
        xf + jnp.einsum("mpd,de->mpe", attended, w_o, preferred_element_type=jnp.float32)
    ).astype(jnp.bfloat16)
    crps_b = crps.astype(jnp.bfloat16)
    dafter = jnp.einsum("mcp,dc->mpd", crps_b, w_out, preferred_element_type=jnp.float32)
    dafter_b = dafter.astype(jnp.bfloat16)
    term_out = jnp.einsum("mpd,mcp->dc", after, crps_b, preferred_element_type=jnp.float32)
    term_o = jnp.einsum("mpd,mpe->de", attended, dafter_b, preferred_element_type=jnp.float32)
    dattend = jnp.einsum("mpe,de->mpd", dafter_b, w_o, preferred_element_type=jnp.float32).astype(
        jnp.bfloat16
    )
    dattend = dattend.reshape(members_here, nblk, BLOCK, heads, HEAD_DIM)
    dprob = jnp.einsum("mnqhd,mnkhd->mnhqk", dattend, vh, preferred_element_type=jnp.float32)
    dval = jnp.einsum("mnhqk,mnqhd->mnkhd", prob_b, dattend, preferred_element_type=jnp.float32)
    delta = jnp.sum(dprob * prob, axis=-1, keepdims=True)
    dscore = (prob * (dprob - delta) * scale).astype(jnp.bfloat16)
    dquery = jnp.einsum("mnhqk,mnkhd->mnqhd", dscore, kh, preferred_element_type=jnp.float32)
    dquery = dquery.reshape(members_here, points, width)
    dkey = jnp.einsum("mnhqk,mnqhd->mnkhd", dscore, qh, preferred_element_type=jnp.float32)
    dwin = jnp.concatenate(
        [
            dkey.reshape(members_here, nblk, 3 * BLOCK, width),
            dval.reshape(members_here, nblk, 3 * BLOCK, width),
        ],
        axis=-1,
    )
    dwin = dwin.reshape(members_here, nblk, 3, BLOCK, 2 * width)
    dwide = jnp.pad(dwin[:, :, 0], ((0, 0), (0, 2), (0, 0), (0, 0)))
    dwide = dwide + jnp.pad(dwin[:, :, 1], ((0, 0), (1, 1), (0, 0), (0, 0)))
    dwide = dwide + jnp.pad(dwin[:, :, 2], ((0, 0), (2, 0), (0, 0), (0, 0)))
    owned = dwide[:, 1:-1].reshape(members_here, points, 2 * width)
    sides = jnp.concatenate([dwide[:, 0], dwide[:, -1]], axis=1)
    returned = extended(sides, (("space", 1),), BLOCK)
    owned = owned.at[:, :BLOCK].add(returned[:, :BLOCK])
    owned = owned.at[:, points - BLOCK :].add(returned[:, 3 * BLOCK :])
    dqkv = jnp.concatenate([dquery, owned], axis=-1).astype(jnp.bfloat16)
    term_qkv = jnp.einsum("mpd,mpe->de", xn, dqkv, preferred_element_type=jnp.float32)
    dnorm = jnp.einsum("mpe,de->mpd", dqkv, w_qkv, preferred_element_type=jnp.float32)
    dlayer = rstd * (
        dnorm
        - jnp.mean(dnorm, axis=-1, keepdims=True)
        - norm * jnp.mean(dnorm * norm, axis=-1, keepdims=True)
    )
    grad_latent = (dafter + dlayer).astype(jnp.bfloat16)
    grad_qkv, grad_o, grad_out = (
        lax.psum_scatter(term_qkv, ("member", "space"), scatter_dimension=0, tiled=True),
        lax.psum_scatter(term_o, ("member", "space"), scatter_dimension=0, tiled=True),
        lax.psum_scatter(term_out, ("member", "space"), scatter_dimension=0, tiled=True),
    )
    return (grad_latent, grad_qkv, grad_o, grad_out)


def solution(mesh):
    placed = (
        P("member", "space", None),
        P("member", None, "space"),
        P(None, "space"),
        P("space"),
        P("space"),
        P(),
        P(),
        P(),
    )
    return jax.shard_map(
        on_device,
        mesh=mesh,
        in_specs=placed,
        out_specs=(
            P("member", "space", None),
            P(("member", "space"), None),
            P(("member", "space"), None),
            P(("member", "space"), None),
        ),
        check_vma=False,
    )
```

profile of v0, /device:TPU:1, one launch (start us, length us, event | category | flops | bytes accessed | tf_op | source)
XLA Modules:
  0.0 1569.3 jit_solution(7611808518516498769)
XLA Ops:
  7.2 0.0 copy-start
  7.2 0.0 all-reduce.6.cloned.1.call-start
  7.2 1.3 convert_reduce_fusion
  8.6 1.3 fusion.66
  9.9 4.9 fusion.16
  14.8 0.0 copy-start.12
  14.8 0.1 slice.90
  14.9 0.0 copy-start.15
  14.9 0.0 copy-start.14
  14.9 3.5 collective-permute-start.1
  18.4 3.5 collective-permute-start
  21.9 0.8 slice.95
  23.4 53.4 %all_gather.3 = f32[16,100,128]{2,1,0:T(8,128)S(1)} all-gather(f32[2,100,128]{2,1,0:T(8,128)S(1)} %copy.54), channel_id=1, replica_groups=mesh['member'=8,'space'=16] {'member'}, dimensions={0}, use_global_device_ids=true | all-gather | bytes 921600 | tf_op jit(solution)/shard_map/all_gather | solution.py:35
  76.8 1.1 copy.57
  77.9 2.1 copy.59
  80.0 1.8 sign_reduce_fusion
  81.8 0.1 multiply_convert_fusion.1
  81.9 0.0 collective-permute-done
  81.9 1.7 pad_maximum_fusion
  83.6 0.4 fusion.95
  84.0 0.4 pad_maximum_fusion.1
  84.4 2.0 fusion.94
  86.4 2.7 copy.61
  89.1 2.6 copy.58
  91.7 6.1 fusion.96
  97.7 4.9 fusion.53
  102.6 0.0 copy-start.9
  102.6 0.0 copy-start.13
  102.7 1.8 convolution_bitcast_fusion.3
  104.5 0.0 all-reduce.6.cloned.1.call-update
  104.5 0.0 reduce-scatter.5.cloned.1.call-start
  104.6 0.3 fusion.75
  104.9 3.8 convolution_bitcast_fusion.1
  108.7 0.0 reduce-scatter.5.cloned.1.call-update
  108.7 0.2 reduce-scatter.3.cloned.1.call-start
  109.0 1.5 fusion.47
  110.5 1.3 copy.60
  111.8 5.4 convolution_bitcast_fusion.2
  117.2 5.8 concatenate.25
  123.0 5.1 copy.63
  128.0 3.7 fusion.97
  131.7 32.1 %fusion.36 = f32[2,1,384,16,64]{2,4,3,0,1:T(8,128)} fusion(bf16[2,128,16,64]{1,3,2,0:T(8,128)(2,1)} %bitcast.105, f32[2,16,128,384]{3,2,1,0:T(8,128)} %fusion.97, f32[2,16,128,384]{3,2,1,0:T(8,128)} %get-tuple-element.57, f32[2,16,128]{2,1,0:T(8,128)S(1)} %get-tuple-element.56), kind=kOutput, calls=%fused_computation.46 | convolution fusion | flops 212341120 | bytes 16269312 | tf_op jit(solution)/shard_map/mnhqk,mnqhd->mnkhd/dot_general | solution.py:86
  163.8 5.7 concatenate.24
  169.6 4.9 copy.62
  174.5 3.3 fusion.27
  177.8 0.4 pad_add_fusion
  178.3 2.3 slice_bitcast_fusion.1
  180.5 1.7 copy-done.2
  182.2 1.9 collective-permute-start.2
  184.1 4.0 collective-permute-start.3
  188.1 31.4 %fusion.50 = bf16[2,16,64,128]{3,2,1,0:T(8,128)(2,1)} fusion(bf16[2,384,16,64]{1,3,2,0:T(8,128)(2,1)S(1)} %bitcast.104, f32[2,16,128,384]{3,2,1,0:T(8,128)} %fusion.97, f32[2,16,128,384]{3,2,1,0:T(8,128)} %get-tuple-element.57, f32[2,16,128]{2,1,0:T(8,128)S(1)} %get-tuple-element.56), kind=kOutput, calls=%fused_computation.58 | convolution fusion | flops 212603264 | bytes 14696448 | tf_op jit(solution)/shard_map/mnhqk,mnkhd->mnqhd/dot_general | solution.py:84
  219.5 1.2 copy.64
  220.8 0.0 copy-start.8
  220.8 0.0 copy-start.4
  220.8 9.3 collective-permute-done.2
  230.1 3.3 fusion.30
  233.5 6.5 convolution_bitcast_fusion
  240.0 0.0 reduce-scatter.3.cloned.1.call-update
  240.0 29.2 %all-reduce.6.cloned.1.call-done = f32[1024,100]{1,0:T(8,128)} async-done(((f32[1024,100]{1,0:T(8,128)}), f32[1024,100]{1,0:T(8,128)}) %all-reduce.6.cloned.1.call-update) | async-done | bytes 409616
  269.2 1.3 constant_dynamic-slice_fusion
  270.5 5.4 fusion.93
  275.9 1.2 fusion.65
  277.1 631.2 %reduce-scatter.5.cloned.1.call-done = f32[8,1024]{1,0:T(8,128)} async-done(((f32[1024,1024]{1,0:T(8,128)}), f32[8,1024]{1,0:T(8,128)}) %reduce-scatter.5.cloned.1.call-update) | async-done | bytes 32784 | tf_op jit(solution)/shard_map/reduce_scatter | solution.py:114
  908.3 654.4 %reduce-scatter.3.cloned.1.call-done = f32[8,3072]{1,0:T(8,128)} async-done(((f32[1024,3072]{1,0:T(8,128)}), f32[8,3072]{1,0:T(8,128)}) %reduce-scatter.3.cloned.1.call-update) | async-done | bytes 98320 | tf_op jit(solution)/shard_map/reduce_scatter | solution.py:113
  (31 shorter events, 0.1 us)
Async XLA Ops:
  7.2 95.5 %copy-start = (bf16[1024,1024]{1,0:T(8,128)(2,1)S(1)}, bf16[1024,1024]{1,0:T(8,128)(2,1)}, u32[]{:S(2)}) copy-start(bf16[1024,1024]{1,0:T(8,128)(2,1)} %param.22) | copy-start | bytes 6291460
  7.2 262.0 %all-reduce.6.cloned.1.call-start = ((), (), s32[]{:S(2)}) async-start(), calls=%async_computation.4 | async-start | bytes 1048576
  14.8 8.6 copy-start.12
  14.9 66.9 %copy-start.15 = (f32[128]{0:T(128)S(1)}, f32[128]{0:T(128)}, u32[]{:S(2)}) copy-start(f32[128]{0:T(128)} %param.19) | copy-start | bytes 1540
  14.9 66.9 %copy-start.14 = (f32[100,128]{1,0:T(8,128)S(1)}, f32[100,128]{1,0:T(8,128)}, u32[]{:S(2)}) copy-start(f32[100,128]{1,0:T(8,128)} %param.18) | copy-start | bytes 153604
  14.9 67.0 %collective-permute-start.1 = (bf16[2,128,2048]{2,1,0:T(8,128)(2,1)S(1)}, bf16[2,128,2048]{2,1,0:T(8,128)(2,1)}, u32[]{:S(2)}, u32[]{:S(2)}) collective-permute-start(bf16[2,128,2048]{2,1,0:T(8,128)(2,1)S(1)} %slice.90), channel_id=1, source_target_pairs={{1,0},{2,1},{3,2},{4,3},{5,4},{6,5},{7,6},{8,7},{9,8},{10,9},{11,1... | collective-permute-start | bytes 3145736 | tf_op jit(solution)/shard_map/ppermute | solution.py:18
  18.4 63.5 %collective-permute-start = (bf16[2,128,2048]{2,1,0:T(8,128)(2,1)S(1)}, bf16[2,128,2048]{2,1,0:T(8,128)(2,1)}, u32[]{:S(2)}, u32[]{:S(2)}) collective-permute-start(bf16[2,128,2048]{2,1,0:T(8,128)(2,1)S(1)} %slice.90), channel_id=1, source_target_pairs={{0,1},{1,2},{2,3},{3,4},{4,5},{5,6},{6,7},{7,8},{8,9},{9,10},{10,1... | collective-permute-start | bytes 3145736 | tf_op jit(solution)/shard_map/ppermute | solution.py:17
  86.4 5.3 copy-start.11
  97.7 4.9 copy-start.3
  102.6 1.9 copy-start.9
  102.6 2.0 copy-start.13
  104.5 803.8 %reduce-scatter.5.cloned.1.call-start = ((), (), s32[]{:S(2)}) async-start(), calls=%async_computation.3 | async-start | bytes 4227072 | tf_op jit(solution)/shard_map/reduce_scatter | solution.py:114
  108.7 1454.0 %reduce-scatter.3.cloned.1.call-start = ((), (), s32[]{:S(2)}) async-start(), calls=%async_computation.2 | async-start | bytes 12681216 | tf_op jit(solution)/shard_map/reduce_scatter | solution.py:113
  123.0 5.1 copy-start.6
  178.3 3.9 copy-start.2
  178.3 9.8 copy-start.10
  182.2 47.9 %collective-permute-start.2 = (f32[2,128,2048]{2,1,0:T(8,128)}, f32[2,128,2048]{2,1,0:T(8,128)}, u32[]{:S(2)}, u32[]{:S(2)}) collective-permute-start(f32[2,128,2048]{2,1,0:T(8,128)} %get-tuple-element.46), channel_id=1, source_target_pairs={{0,1},{1,2},{2,3},{3,4},{4,5},{5,6},{6,7},{7,8},{8,9},{9,10},{10,1... | collective-permute-start | bytes 6291464 | tf_op jit(solution)/shard_map/ppermute | solution.py:17
  184.1 46.0 %collective-permute-start.3 = (f32[2,128,2048]{2,1,0:T(8,128)}, f32[2,128,2048]{2,1,0:T(8,128)}, u32[]{:S(2)}, u32[]{:S(2)}) collective-permute-start(f32[2,128,2048]{2,1,0:T(8,128)} %get-tuple-element.47), channel_id=1, source_target_pairs={{1,0},{2,1},{3,2},{4,3},{5,4},{6,5},{7,6},{8,7},{9,8},{10,9},{11,1... | collective-permute-start | bytes 6291464 | tf_op jit(solution)/shard_map/ppermute | solution.py:18
  220.8 12.7 copy-start.8
  220.8 12.7 copy-start.4
  233.5 6.5 copy-start.7
  270.5 5.4 copy-start.5
  270.5 1292.3 %copy-start.1 = (bf16[1024,1024]{1,0:T(8,128)(2,1)S(1)}, bf16[1024,1024]{1,0:T(8,128)(2,1)}, u32[]{:S(2)}) copy-start(bf16[1024,1024]{1,0:T(8,128)(2,1)} %param.22) | copy-start | bytes 6291460
Sparse Core Ops, SparseCore 0:
  104.7 164.5 all-reduce.5
  272.3 636.0 reduce-scatter.4
  911.3 651.4 reduce-scatter.2
where the time goes:
time: 1580 us; the launch traced here: 1570 us
  waiting for transfers between devices  1320 us (84%)
  matrix products  108 us (7%)
  blocking collectives  53.4 us (3%)
  local copies, waits for them, and re-layouts  41 us (3%)
    reduce_scatter x1, waiting for transfers between devices, on_device(): lax.psum_scatter(term_qkv, ('member', 'space'), scatter_dimension=0, tile...  654 us
    reduce_scatter x1, waiting for transfers between devices, on_device(): lax.psum_scatter(term_o, ('member', 'space'), scatter_dimension=0, tiled=...  631 us
    all_gather x1, blocking collectives, on_device(): every = lax.all_gather(predictions, 'member', axis=0, tiled=True)  53.4 us
    dot_general x1, matrix products, on_device(): jnp.einsum('mnhqk,mnqhd->mnkhd', dscore, qh, preferred_element_type=jnp.f...  32.1 us
  transfers between devices with their start and end apart: 7, of which 4 were waited for; matrix products, arithmetic and copies ran while one was open for 8% of the time, Pallas kernels for 0%

commit v1 on v0

--- a/solution.py
+++ b/solution.py
@@ -1,10 +1,267 @@
+import functools
+
 import jax
 import jax.numpy as jnp
 from jax import lax
+from jax.experimental import pallas as pl
+from jax.experimental.pallas import tpu as pltpu
 from jax.sharding import PartitionSpec as P
 
 HEAD_DIM = 64
 BLOCK = 128
+RING = 4
+F32 = jnp.float32
+BF16 = jnp.bfloat16
+
+ORDERS = (("x", "y", "z"), ("y", "z", "x"), ("z", "x", "y"))
+WIDTHS = (640, 768, 768)
+
+
+class Place:
+    def __init__(self):
+        self.member = lax.axis_index("member")
+        self.space = lax.axis_index("space")
+        self.core = self.space % 2
+        z_lo = (self.space // 2) % 2
+        z_hi = self.member % 2
+        self.at = {"x": self.space // 4, "y": self.member // 2, "z": z_hi * 2 + z_lo}
+
+    def partner(self, axis, index):
+        if axis == "x":
+            return (self.member, index * 4 + self.space % 4)
+        if axis == "y":
+            return (index * 2 + self.member % 2, self.space)
+        member = (self.member // 2) * 2 + index // 2
+        return (member, (self.space // 4) * 4 + (index % 2) * 2 + self.core)
+
+    def pair(self):
+        return (self.member, self.space + 1 - 2 * self.core)
+
+    def ahead(self, axis, offset):
+        return (self.at[axis] + offset) % RING
+
+
+def chunk_order(order):
+    where = []
+    for y in range(4):
+        for z_hi in range(2):
+            for x in range(4):
+                for z_lo in range(2):
+                    digit = {"x": x, "y": y, "z": z_hi * 2 + z_lo}
+                    a, b, c = (digit[name] for name in order)
+                    where.append(a * 16 + b * 4 + c)
+    return where
+
+
+def remote(src, dst, send, recv, device):
+    return pltpu.make_async_remote_copy(
+        src_ref=src,
+        dst_ref=dst,
+        send_sem=send,
+        recv_sem=recv,
+        device_id=device,
+        device_id_type=pl.DeviceIdType.MESH,
+    )
+
+
+def dot(a, b):
+    return jnp.dot(a, b, preferred_element_type=F32)
+
+
+def reduce_kernel(
+    xn, dqkv, att, daf, aft, crps, g_qkv, g_o, g_out,
+    xn_o, att_o, d_q, d_k, d_v, d_o, xt_a, xt_b, xt_c, at_b, at_c, ft_a,
+    send1_a, send1_b, send1_c, recv1_a, recv1_b, recv1_c, acc1_a, acc1_b, acc1_c,
+    send2_a, send2_b, send2_c, recv2_a, recv2_b, recv2_c, acc2_a, acc2_b, acc2_c,
+    recv3_a, recv3_b, recv3_c, fin_a, fin_b, fin_c, oth_a, oth_b, oth_c,
+    pair_send, pair_recv, ring_send, ring_recv, last_send, last_recv,
+):
+    place = Place()
+    core = place.core
+    rows = xn.shape[0]
+    half = 512
+
+    barrier = pltpu.get_barrier_semaphore()
+    pl.semaphore_signal(barrier, inc=1, device_id=place.pair(), device_id_type=pl.DeviceIdType.MESH)
+    for axis in ("x", "y", "z"):
+        for offset in (1, 2, 3):
+            pl.semaphore_signal(
+                barrier, inc=1, device_id=place.partner(axis, place.ahead(axis, offset)),
+                device_id_type=pl.DeviceIdType.MESH,
+            )
+    pl.semaphore_wait(barrier, 10)
+
+    theirs = pl.multiple_of((1 - core) * half, half)
+    moves = [
+        (xn, xn_o),
+        (dqkv.at[:, pl.ds(theirs, half)], d_q.at[pl.ds(rows, rows)]),
+        (dqkv.at[:, pl.ds(1024 + theirs, half)], d_k.at[pl.ds(rows, rows)]),
+        (dqkv.at[:, pl.ds(2048 + theirs, half)], d_v.at[pl.ds(rows, rows)]),
+        (att, att_o),
+        (daf.at[:, pl.ds(theirs, half)], d_o.at[pl.ds(rows, rows)]),
+    ]
+    pair = [
+        remote(src, dst, pair_send.at[i], pair_recv.at[i], place.pair())
+        for i, (src, dst) in enumerate(moves)
+    ]
+    for copy in pair:
+        copy.start()
+
+    def mine(ref, start):
+        return jnp.where(core == 0, ref[:, start : start + half], ref[:, start + half : start + 2 * half])
+
+    d_q[:rows] = mine(dqkv, 0)
+    d_k[:rows] = mine(dqkv, 1024)
+    d_v[:rows] = mine(dqkv, 2048)
+    d_o[:rows] = mine(daf, 0)
+
+    def lay(value, targets, column):
+        turned = value.T
+        for ref, order in targets:
+            for chunk, spot in enumerate(chunk_order(order)):
+                ref[spot * 16 : spot * 16 + 16, column : column + rows] = turned[chunk * 16 : chunk * 16 + 16]
+
+    xts = [(xt_a, ORDERS[0]), (xt_b, ORDERS[1]), (xt_c, ORDERS[2])]
+    ats = [(at_b, ORDERS[1]), (at_c, ORDERS[2])]
+    lay(xn[...], xts, 0)
+    lay(att[...], ats, 0)
+    lay(aft[...], [(ft_a, ORDERS[0])], 0)
+    pair[0].wait_recv()
+    lay(xn_o[...], xts, rows)
+    pair[4].wait_recv()
+    lay(att_o[...], ats, rows)
+    for i in (1, 2, 3, 5):
+        pair[i].wait_recv()
+
+    def part(p, dest):
+        rows_of = pl.ds(pl.multiple_of(dest * 256, 256), 256)
+        if p == 0:
+            return (dot(xt_a[rows_of], d_q[...]), dot(ft_a[rows_of], crps[...]))
+        if p == 1:
+            return (dot(xt_b[rows_of], d_k[...]), dot(at_b[rows_of], d_o[:, :256]))
+        return (dot(xt_c[rows_of], d_v[...]), dot(at_c[rows_of], d_o[:, 256:]))
+
+    send1, recv1, acc1 = (send1_a, send1_b, send1_c), (recv1_a, recv1_b, recv1_c), (acc1_a, acc1_b, acc1_c)
+    send2, recv2, acc2 = (send2_a, send2_b, send2_c), (recv2_a, recv2_b, recv2_c), (acc2_a, acc2_b, acc2_c)
+    recv3, fin, oth = (recv3_a, recv3_b, recv3_c), (fin_a, fin_b, fin_c), (oth_a, oth_b, oth_c)
+    started = []
+
+    def push(p, phase, offset, src, dst):
+        axis = ORDERS[p][phase]
+        slot = p * 9 + phase * 3 + offset - 1
+        copy = remote(
+            src, dst, ring_send.at[slot], ring_recv.at[slot],
+            place.partner(axis, place.ahead(axis, offset)),
+        )
+        copy.start()
+        started.append(copy)
+        return copy
+
+    first = {}
+    for offset in (2, 1, 3):
+        for p in range(3):
+            left, right = part(p, place.ahead(ORDERS[p][0], offset))
+            send1[p][offset - 1, :, :half] = left.astype(BF16)
+            send1[p][offset - 1, :, half:] = right.astype(BF16)
+            first[p, offset] = push(p, 0, offset, send1[p].at[offset - 1], recv1[p].at[offset - 1])
+    for p in range(3):
+        left, right = part(p, place.at[ORDERS[p][0]])
+        acc1[p][:, :half] = left
+        acc1[p][:, half:] = right
+    second = {}
+    for p in range(3):
+        for offset in (1, 2, 3):
+            first[p, offset].wait_recv()
+        acc1[p][...] += (
+            recv1[p][0].astype(F32) + recv1[p][1].astype(F32) + recv1[p][2].astype(F32)
+        )
+        for offset in (2, 1, 3):
+            dest = place.ahead(ORDERS[p][1], offset)
+            send2[p][offset - 1] = acc1[p][pl.ds(pl.multiple_of(dest * 64, 64), 64)].astype(BF16)
+            second[p, offset] = push(p, 1, offset, send2[p].at[offset - 1], recv2[p].at[offset - 1])
+    third = {}
+    for p in range(3):
+        for offset in (1, 2, 3):
+            second[p, offset].wait_recv()
+        own = acc1[p][pl.ds(pl.multiple_of(place.at[ORDERS[p][1]] * 64, 64), 64)]
+        acc2[p][...] = own + (
+            recv2[p][0].astype(F32) + recv2[p][1].astype(F32) + recv2[p][2].astype(F32)
+        )
+        for offset in (2, 1, 3):
+            dest = place.ahead(ORDERS[p][2], offset)
+            src = acc2[p].at[pl.ds(pl.multiple_of(dest * 16, 16), 16)]
+            third[p, offset] = push(p, 2, offset, src, recv3[p].at[offset - 1])
+    last = []
+    for p in range(3):
+        for offset in (1, 2, 3):
+            third[p, offset].wait_recv()
+        own = acc2[p][pl.ds(pl.multiple_of(place.at[ORDERS[p][2]] * 16, 16), 16)]
+        fin[p][...] = own + recv3[p][0] + recv3[p][1] + recv3[p][2]
+        copy = remote(
+            fin[p].at[pl.ds(pl.multiple_of((1 - core) * 8, 8), 8)], oth[p],
+            last_send.at[p], last_recv.at[p], place.pair(),
+        )
+        copy.start()
+        last.append(copy)
+    keep = pl.ds(pl.multiple_of(core * 8, 8), 8)
+
+    def both(own, other):
+        return jnp.where(core == 0, own, other), jnp.where(core == 0, other, own)
+
+    for p in range(3):
+        last[p].wait_recv()
+        low, high = both(fin[p][keep, :half], oth[p][:, :half])
+        g_qkv[:, p * 1024 : p * 1024 + half] = low
+        g_qkv[:, p * 1024 + half : p * 1024 + 2 * half] = high
+        if p == 0:
+            g_out[...] = fin[p][keep, half:] + oth[p][:, half:]
+        else:
+            low, high = both(fin[p][keep, half:], oth[p][:, half:])
+            g_o[:, (p - 1) * 256 : p * 256] = low
+            g_o[:, half + (p - 1) * 256 : half + p * 256] = high
+    for copy in pair + started + last:
+        copy.wait_send()
+
+
+def reduce_terms(xn, dqkv, att, daf, aft, crps):
+    rows = xn.shape[0]
+    vmem = pl.BlockSpec(memory_space=pltpu.VMEM)
+    scratch = [
+        pltpu.VMEM((rows, 1024), BF16),
+        pltpu.VMEM((rows, 1024), BF16),
+        *[pltpu.VMEM((2 * rows, 512), BF16)] * 4,
+        *[pltpu.VMEM((1024, 2 * rows), BF16)] * 5,
+        pltpu.VMEM((1024, rows), BF16),
+        *[pltpu.VMEM((3, 256, w), BF16) for w in WIDTHS],
+        *[pltpu.VMEM((3, 256, w), BF16) for w in WIDTHS],
+        *[pltpu.VMEM((256, w), F32) for w in WIDTHS],
+        *[pltpu.VMEM((3, 64, w), BF16) for w in WIDTHS],
+        *[pltpu.VMEM((3, 64, w), BF16) for w in WIDTHS],
+        *[pltpu.VMEM((64, w), F32) for w in WIDTHS],
+        *[pltpu.VMEM((3, 16, w), F32) for w in WIDTHS],
+        *[pltpu.VMEM((16, w), F32) for w in WIDTHS],
+        *[pltpu.VMEM((8, w), F32) for w in WIDTHS],
+        pltpu.SemaphoreType.DMA((6,)),
+        pltpu.SemaphoreType.DMA((6,)),
+        pltpu.SemaphoreType.DMA((27,)),
+        pltpu.SemaphoreType.DMA((27,)),
+        pltpu.SemaphoreType.DMA((3,)),
+        pltpu.SemaphoreType.DMA((3,)),
+    ]
+    return pl.pallas_call(
+        reduce_kernel,
+        out_shape=(
+            jax.ShapeDtypeStruct((8, 3072), F32),
+            jax.ShapeDtypeStruct((8, 1024), F32),
+            jax.ShapeDtypeStruct((8, 128), F32),
+        ),
+        in_specs=[vmem] * 6,
+        out_specs=[vmem] * 3,
+        scratch_shapes=scratch,
+        compiler_params=pltpu.CompilerParams(
+            collective_id=0, has_side_effects=True, vmem_limit_bytes=48 * 1024 * 1024
+        ),
+    )(xn, dqkv, att, daf, aft, crps)
 
 
 def extended(value, sides, width):
@@ -71,8 +328,6 @@
     crps_b = crps.astype(jnp.bfloat16)
     dafter = jnp.einsum("mcp,dc->mpd", crps_b, w_out, preferred_element_type=jnp.float32)
     dafter_b = dafter.astype(jnp.bfloat16)
-    term_out = jnp.einsum("mpd,mcp->dc", after, crps_b, preferred_element_type=jnp.float32)
-    term_o = jnp.einsum("mpd,mpe->de", attended, dafter_b, preferred_element_type=jnp.float32)
     dattend = jnp.einsum("mpe,de->mpd", dafter_b, w_o, preferred_element_type=jnp.float32).astype(
         jnp.bfloat16
     )
@@ -101,7 +356,6 @@
     owned = owned.at[:, :BLOCK].add(returned[:, :BLOCK])
     owned = owned.at[:, points - BLOCK :].add(returned[:, 3 * BLOCK :])
     dqkv = jnp.concatenate([dquery, owned], axis=-1).astype(jnp.bfloat16)
-    term_qkv = jnp.einsum("mpd,mpe->de", xn, dqkv, preferred_element_type=jnp.float32)
     dnorm = jnp.einsum("mpe,de->mpd", dqkv, w_qkv, preferred_element_type=jnp.float32)
     dlayer = rstd * (
         dnorm
@@ -109,11 +363,14 @@
         - norm * jnp.mean(dnorm * norm, axis=-1, keepdims=True)
     )
     grad_latent = (dafter + dlayer).astype(jnp.bfloat16)
-    grad_qkv, grad_o, grad_out = (
-        lax.psum_scatter(term_qkv, ("member", "space"), scatter_dimension=0, tiled=True),
-        lax.psum_scatter(term_o, ("member", "space"), scatter_dimension=0, tiled=True),
-        lax.psum_scatter(term_out, ("member", "space"), scatter_dimension=0, tiled=True),
-    )
+    rows = members_here * points
+    channels = crps_b.shape[1]
+    crps_rows = jnp.pad(crps_b.transpose(0, 2, 1).reshape(rows, channels), ((0, 0), (0, 128 - channels)))
+    grad_qkv, grad_o, grad_out = reduce_terms(
+        xn.reshape(rows, width), dqkv.reshape(rows, 3 * width), attended.reshape(rows, width),
+        dafter_b.reshape(rows, width), after.reshape(rows, width), crps_rows,
+    )
+    grad_out = grad_out[:, :channels]
     return (grad_latent, grad_qkv, grad_o, grad_out)
 
 

time: 1580 us -> 281 us (0.18)
  waiting for transfers between devices: 1320 us -> 0.01 us
  Pallas kernels: 0 us -> 42.2 us
    reduce_scatter x2 -> x0, waiting for transfers between devices: 1290 us -> none  [the longest x1 654 us: on_device(): lax.psum_scatter(term_qkv, ('member', 'space'), scatter_dimension=0, tile...]
    pallas_call x0 -> x1, Pallas kernels: none -> 42.2 us  [reduce_terms(): pl.pallas_call(reduce_kernel, out_shape=(jax.ShapeDtypeStruct((8, 3072),...]
    unnamed x4 -> x0, waiting for transfers between devices: 29.3 us -> none
  transfers between devices with their start and end apart: 7 -> 4, of which waited for: 4 -> 0; matrix products, arithmetic and copies ran while one was open for 8% -> 20% of each run, Pallas kernels for 0% -> 0%
where the time goes in v1:
time: 281 us; the launch traced here: 280 us
  matrix products  97.7 us (35%)
  blocking collectives  54.4 us (19%)
  local copies, waits for them, and re-layouts  51.5 us (18%)
  Pallas kernels  42.2 us (15%)
  other arithmetic  20.1 us (7%)
  starting transfers between devices  12.4 us (4%)
    all_gather x1, blocking collectives, on_device(): every = lax.all_gather(predictions, 'member', axis=0, tiled=True)  54.4 us
    pallas_call x1, Pallas kernels, reduce_terms(): pl.pallas_call(reduce_kernel, out_shape=(jax.ShapeDtypeStruct((8, 3072),...  42.2 us
    dot_general x1, matrix products, on_device(): jnp.einsum('mnhqk,mnqhd->mnkhd', dscore, qh, preferred_element_type=jnp.f...  32.1 us
    dot_general x1, matrix products, on_device(): jnp.einsum('mnhqk,mnkhd->mnqhd', dscore, kh, preferred_element_type=jnp.f...  31.4 us
    concatenate x4, local copies, waits for them, and re-layouts, on_device(): jnp.concatenate([dkey.reshape(members_here, nblk, 3 * BLOCK, width), dval...  21.3 us
    ppermute x2, starting transfers between devices, extended(): before = lax.ppermute(last, axis, up)  7.17 us
    sub x1, matrix products, on_device(): prob = jax.nn.softmax(scores, axis=-1)  6.22 us
    another operation x2, other arithmetic  6.21 us
  transfers between devices with their start and end apart: 4, of which 0 were waited for; matrix products, arithmetic and copies ran while one was open for 20% of the time, Pallas kernels for 0%

profile of v1, /device:TPU:1, one launch (start us, length us, event | category | flops | bytes accessed | tf_op | source)
XLA Modules:
  0.0 280.0 jit_solution(4518135686213898549)
XLA Ops:
  0.6 0.0 copy-start
  0.6 1.3 convert_reduce_fusion
  2.0 1.3 fusion.69
  3.3 1.3 fusion.63
  4.6 4.8 %fusion.16 = bf16[2,128,3072]{2,1,0:T(8,128)(2,1)S(1)} fusion(bf16[2,128,1024]{2,1,0:T(8,128)(2,1)S(1)} %fusion.63, bf16[1024,3072]{1,0:T(8,128)(2,1)} %param.21), kind=kOutput, calls=%fused_computation.19 | convolution fusion | flops 1611399168 | bytes 8388608 | tf_op jit(solution)/shard_map/mpd,de->mpe/dot_general | solution.py:301
  9.4 0.0 copy-start.12
  9.4 1.1 slice.94
  10.5 3.3 %collective-permute-start.1 = (bf16[2,128,2048]{2,1,0:T(8,128)(2,1)}, bf16[2,128,2048]{2,1,0:T(8,128)(2,1)}, u32[]{:S(2)}, u32[]{:S(2)}) collective-permute-start(bf16[2,128,2048]{2,1,0:T(8,128)(2,1)} %slice.94), channel_id=1, source_target_pairs={{1,0},{2,1},{3,2},{4,3},{5,4},{6,5},{7,6},{8,7},{9,8},{10,9},{11,1... | collective-permute-start | bytes 3145736 | tf_op jit(solution)/shard_map/ppermute | solution.py:275
  13.8 3.5 %collective-permute-start = (bf16[2,128,2048]{2,1,0:T(8,128)(2,1)}, bf16[2,128,2048]{2,1,0:T(8,128)(2,1)}, u32[]{:S(2)}, u32[]{:S(2)}) collective-permute-start(bf16[2,128,2048]{2,1,0:T(8,128)(2,1)} %slice.94), channel_id=1, source_target_pairs={{0,1},{1,2},{2,3},{3,4},{4,5},{5,6},{6,7},{7,8},{8,9},{9,10},{10,1... | collective-permute-start | bytes 3145736 | tf_op jit(solution)/shard_map/ppermute | solution.py:274
  18.1 54.4 %all_gather.3 = f32[16,100,128]{2,1,0:T(8,128)S(1)} all-gather(f32[2,100,128]{2,1,0:T(8,128)S(1)} %copy.60), channel_id=1, replica_groups=mesh['member'=8,'space'=16] {'member'}, dimensions={0}, use_global_device_ids=true | all-gather | bytes 921600 | tf_op jit(solution)/shard_map/all_gather | solution.py:292
  72.5 0.2 copy.63
  72.6 1.0 copy.65
  73.6 0.7 compare_select_fusion
  74.3 0.7 sign_reduce_fusion
  75.0 1.0 multiply_convert_fusion.1
  76.0 2.2 fusion.93
  78.2 1.5 fusion.50
  79.7 1.3 copy.66
  81.1 0.0 collective-permute-done.1
  81.1 0.0 collective-permute-done
  81.1 2.2 pad_maximum_fusion
  83.3 0.4 fusion.92
  83.7 0.4 pad_maximum_fusion.1
  84.1 2.0 fusion.91
  86.1 2.6 copy.67
  88.7 2.6 copy.64
  91.3 5.0 %fusion.95 = f32[2,16,128,384]{3,2,1,0:T(8,128)} fusion(bf16[2,128,16,64]{1,3,2,0:T(8,128)(2,1)S(1)} %bitcast.121, bf16[2,384,16,64]{1,3,2,0:T(8,128)(2,1)} %bitcast.117), kind=kOutput, calls=%fused_computation.108 | convolution fusion | flops 201326592 | bytes 8388608 | tf_op jit(solution)/shard_map/mnqhd,mnkhd->mnhqk/dot_general | solution.py:335
  96.3 6.2 %fusion.94 = (f32[2,16,128]{2,1,0:T(8,128)S(1)}, f32[2,16,128,384]{3,2,1,0:T(8,128)}) fusion(pred[384]{0:T(512)(128)(4,1)S(1)} %fusion.80, bf16[2,128,16,64]{1,3,2,0:T(8,128)(2,1)} %bitcast.127, bf16[2,384,16,64]{1,3,2,0:T(8,128)(2,1)} %bitcast.125), kind=kOutput, calls=%fused_computation.107 | convolution fusion | flops 207618432 | bytes 8405376 | tf_op jit(solution)/shard_map/sub | solution.py:321
  102.6 5.2 %convolution_bitcast_fusion = f32[2,1,384,16,64]{2,4,3,0,1:T(8,128)} fusion(bf16[2,128,16,64]{1,3,2,0:T(8,128)(2,1)S(1)} %bitcast.122, f32[2,16,128,384]{3,2,1,0:T(8,128)} %get-tuple-element.66, f32[2,16,128]{2,1,0:T(8,128)S(1)} %get-tuple-element.65), kind=kOutput, calls=%fused_computation.47 | convolution fusion | flops 204472320 | bytes 9977856 | tf_op jit(solution)/shard_map/mnhqk,mnqhd->mnkhd/dot_general | solution.py:336
  107.8 32.1 %fusion.36 = f32[2,1,384,16,64]{2,4,3,0,1:T(8,128)} fusion(bf16[2,128,16,64]{1,3,2,0:T(8,128)(2,1)} %bitcast.128, f32[2,16,128,384]{3,2,1,0:T(8,128)} %fusion.95, f32[2,16,128,384]{3,2,1,0:T(8,128)} %get-tuple-element.66, f32[2,16,128]{2,1,0:T(8,128)S(1)} %get-tuple-element.65), kind=kOutput, calls=%fused_computation.46 | convolution fusion | flops 212341120 | bytes 16269312 | tf_op jit(solution)/shard_map/mnhqk,mnqhd->mnkhd/dot_general | solution.py:341
  139.9 5.7 %concatenate.31 = f32[2,1,3,128,1024]{3,2,4,0,1:T(4,128)} reshape(f32[2,1,384,16,64]{2,4,3,0,1:T(8,128)} %convolution_bitcast_fusion) | data formatting | bytes 6291456 | tf_op jit(solution)/shard_map/concatenate | solution.py:342
  145.6 4.9 %copy.69 = f32[2,1,3,128,1024]{4,3,0,2,1:T(8,128)} copy(f32[2,1,3,128,1024]{3,2,4,0,1:T(4,128)} %concatenate.31) | data formatting | bytes 6291456 | tf_op jit(solution)/shard_map/concatenate | solution.py:342
  150.5 5.7 %concatenate.30 = f32[2,1,3,128,1024]{3,2,4,0,1:T(4,128)} reshape(f32[2,1,384,16,64]{2,4,3,0,1:T(8,128)} %fusion.36) | data formatting | bytes 6291456 | tf_op jit(solution)/shard_map/concatenate | solution.py:342
  156.2 4.9 %copy.68 = f32[2,1,3,128,1024]{4,3,0,2,1:T(8,128)} copy(f32[2,1,3,128,1024]{3,2,4,0,1:T(4,128)} %concatenate.30) | data formatting | bytes 6291456 | tf_op jit(solution)/shard_map/concatenate | solution.py:342
  161.2 3.2 %fusion.27 = (f32[2,1,128,2048]{3,2,0,1:T(8,128)S(1)}, f32[2,1,128,2048]{3,2,0,1:T(8,128)S(1)}, f32[2,1,128,2048]{3,2,0,1:T(8,128)S(1)}) fusion(f32[2,1,3,128,1024]{4,3,0,2,1:T(8,128)} %copy.68, f32[2,1,3,128,1024]{4,3,0,2,1:T(8,128)} %copy.69), kind=kLoop, calls=%fused_computation.31 | loop fusion | flops 1572864 | bytes 12582912 | tf_op jit(solution)/shard_map/squeeze | solution.py:350
  164.4 0.4 pad_add_fusion
  164.8 2.9 %fusion.90 = (f32[2,1,128,2048]{3,2,0,1:T(8,128)}, f32[2,128,2048]{2,1,0:T(8,128)}, f32[2,128,2048]{2,1,0:T(8,128)}) fusion(f32[2,3,128,2048]{3,2,0,1:T(8,128)S(1)} %pad_add_fusion), kind=kLoop, calls=%fused_computation.103 | loop fusion | bytes 12582912 | tf_op jit(solution)/shard_map/slice | solution.py:353
  167.8 1.6 copy-done.3
  169.4 1.9 collective-permute-start.3
  171.3 3.6 %collective-permute-start.2 = (f32[2,128,2048]{2,1,0:T(8,128)}, f32[2,128,2048]{2,1,0:T(8,128)}, u32[]{:S(2)}, u32[]{:S(2)}) collective-permute-start(f32[2,128,2048]{2,1,0:T(8,128)} %get-tuple-element.54), channel_id=1, source_target_pairs={{0,1},{1,2},{2,3},{3,4},{4,5},{5,6},{6,7},{7,8},{8,9},{9,10},{10,1... | collective-permute-start | bytes 6291464 | tf_op jit(solution)/shard_map/ppermute | solution.py:274
  174.9 0.1 copy.75
  175.1 31.4 %fusion.53 = bf16[2,16,64,128]{3,2,1,0:T(8,128)(2,1)S(1)} fusion(bf16[2,384,16,64]{1,3,2,0:T(8,128)(2,1)} %bitcast.126, f32[2,16,128,384]{3,2,1,0:T(8,128)} %fusion.95, f32[2,16,128,384]{3,2,1,0:T(8,128)} %get-tuple-element.66, f32[2,16,128]{2,1,0:T(8,128)S(1)} %get-tuple-element.65), kind=kOutput, calls=%fused_computation.61 | convolution fusion | flops 212603264 | bytes 14696448 | tf_op jit(solution)/shard_map/mnhqk,mnkhd->mnqhd/dot_general | solution.py:339
  206.6 0.8 copy-done.8
  207.3 1.0 copy.70
  208.3 4.9 %fusion.56 = bf16[2,16,64,128]{3,2,1,0:T(8,128)(2,1)S(1)} fusion(bf16[2,384,16,64]{1,3,2,0:T(8,128)(2,1)} %bitcast.118, f32[2,16,128,384]{3,2,1,0:T(8,128)} %get-tuple-element.66, f32[2,16,128]{2,1,0:T(8,128)S(1)} %get-tuple-element.65), kind=kOutput, calls=%fused_computation.62 | convolution fusion | flops 204734464 | bytes 8404992 | tf_op jit(solution)/shard_map/mnhqk,mnkhd->mnqhd/dot_general | solution.py:323
  213.2 0.8 copy-done.7
  214.0 1.8 copy.79
  215.7 1.9 reshape.257.att
  217.7 2.8 copy.78
  220.5 2.6 reshape.256
  223.0 2.1 fusion.47
  225.2 0.0 slice-start.1
  225.2 2.8 %fusion.29 = bf16[256,2048]{1,0:T(8,128)(2,1)S(1)} fusion(f32[2,128,2048]{2,1,0:T(8,128)} %collective-permute-done.3, f32[2,128,2048]{2,1,0:T(8,128)} %collective-permute-done.2, f32[2,1,128,2048]{3,2,0,1:T(8,128)S(1)} %copy-done.5), kind=kLoop, calls=%fused_computation.37 | loop fusion | flops 1572864 | bytes 7340032 | tf_op jit(solution)/shard_map/convert.1
  228.1 0.1 pad_maximum_fusion.3.dqkv
  228.2 0.9 copy-done.2
  229.1 42.2 %shard_map.121 = (f32[8,3072]{1,0:T(8,128)S(1)}, f32[8,1024]{1,0:T(8,128)S(1)}, f32[8,128]{1,0:T(8,128)S(1)}) custom-call(bf16[256,1024]{1,0:T(8,128)(2,1)S(1)} %bitcast.114, bf16[256,3072]{1,0:T(8,128)(2,1)S(1)} %pad_maximum_fusion.3.dqkv, bf16[256,1024]{1,0:T(8,128)(2,1)S(1)} %reshape.257.att, bf16[256,1024]{1,0:T(8,128)(2,1)S(1)} %bitcast.112, ...), custom_call_target="tpu_custom_call" | custom-call | tf_op jit(solution)/shard_map/pallas_call | solution.py:251
  271.3 0.0 copy-start.4
  271.3 0.0 copy-start.11
  271.3 3.4 %fusion.31 = bf16[2,128,2048]{2,1,0:T(8,128)(2,1)S(1)} fusion(f32[2,128,2048]{2,1,0:T(8,128)} %collective-permute-done.3, f32[2,128,2048]{2,1,0:T(8,128)} %collective-permute-done.2, f32[2,3,128,2048]{3,2,0,1:T(8,128)} %copy-done.3), kind=kLoop, calls=%fused_computation.41 | loop fusion | flops 1572864 | bytes 7340032 | tf_op jit(solution)/shard_map/convert.4
  274.8 2.2 fusion.89
  277.0 1.2 fusion.68
  278.2 0.6 copy.87
  278.8 0.6 copy.88
  279.4 0.6 copy.89
  (32 shorter events, 0.1 us)
Async XLA Ops:
  0.6 77.6 %copy-start = (bf16[1024,1024]{1,0:T(8,128)(2,1)S(1)}, bf16[1024,1024]{1,0:T(8,128)(2,1)}, u32[]{:S(2)}) copy-start(bf16[1024,1024]{1,0:T(8,128)(2,1)} %param.22) | copy-start | bytes 6291460
  4.6 4.8 %copy-start.1 = (bf16[2,128,1024]{2,1,0:T(8,128)(2,1)}, bf16[2,128,1024]{2,1,0:T(8,128)(2,1)S(1)}, u32[]{:S(2)}) copy-start(bf16[2,128,1024]{2,1,0:T(8,128)(2,1)S(1)} %fusion.63) | copy-start | bytes 1572868
  9.4 7.9 %copy-start.9 = (bf16[2,128,3072]{2,1,0:T(8,128)(2,1)}, bf16[2,128,3072]{2,1,0:T(8,128)(2,1)S(1)}, u32[]{:S(2)}) copy-start(bf16[2,128,3072]{2,1,0:T(8,128)(2,1)S(1)} %fusion.16) | copy-start | bytes 4718596
  9.4 8.7 %copy-start.12 = (f32[2,100,128]{2,0,1:T(2,128)S(1)}, f32[2,100,128]{2,0,1:T(2,128)}, u32[]{:S(2)}) copy-start(f32[2,100,128]{2,0,1:T(2,128)} %param.17) | copy-start | bytes 307204
  10.5 70.6 %collective-permute-start.1 = (bf16[2,128,2048]{2,1,0:T(8,128)(2,1)}, bf16[2,128,2048]{2,1,0:T(8,128)(2,1)}, u32[]{:S(2)}, u32[]{:S(2)}) collective-permute-start(bf16[2,128,2048]{2,1,0:T(8,128)(2,1)} %slice.94), channel_id=1, source_target_pairs={{1,0},{2,1},{3,2},{4,3},{5,4},{6,5},{7,6},{8,7},{9,8},{10,9},{11,1... | collective-permute-start | bytes 3145736 | tf_op jit(solution)/shard_map/ppermute | solution.py:275
  13.8 67.3 %collective-permute-start = (bf16[2,128,2048]{2,1,0:T(8,128)(2,1)}, bf16[2,128,2048]{2,1,0:T(8,128)(2,1)}, u32[]{:S(2)}, u32[]{:S(2)}) collective-permute-start(bf16[2,128,2048]{2,1,0:T(8,128)(2,1)} %slice.94), channel_id=1, source_target_pairs={{0,1},{1,2},{2,3},{3,4},{4,5},{5,6},{6,7},{7,8},{8,9},{9,10},{10,1... | collective-permute-start | bytes 3145736 | tf_op jit(solution)/shard_map/ppermute | solution.py:274
  17.4 55.3 %slice-start = ((bf16[2,128,3072]{2,1,0:T(8,128)(2,1)}), bf16[2,128,1024]{2,1,0:T(8,128)(2,1)S(1)}, s32[]{:S(2)}) async-start(bf16[2,128,3072]{2,1,0:T(8,128)(2,1)} %copy-done.9), calls=%async_computation | async-start | bytes 1048576 | tf_op jit(solution)/shard_map/slice | solution.py:304
  164.8 4.5 %copy-start.3 = (f32[2,3,128,2048]{3,2,0,1:T(8,128)}, f32[2,3,128,2048]{3,2,0,1:T(8,128)S(1)}, u32[]{:S(2)}) copy-start(f32[2,3,128,2048]{3,2,0,1:T(8,128)S(1)} %pad_add_fusion) | copy-start | bytes 18874372
  169.4 55.8 %collective-permute-start.3 = (f32[2,128,2048]{2,1,0:T(8,128)}, f32[2,128,2048]{2,1,0:T(8,128)}, u32[]{:S(2)}, u32[]{:S(2)}) collective-permute-start(f32[2,128,2048]{2,1,0:T(8,128)} %get-tuple-element.53), channel_id=1, source_target_pairs={{1,0},{2,1},{3,2},{4,3},{5,4},{6,5},{7,6},{8,7},{9,8},{10,9},{11,1... | collective-permute-start | bytes 6291464 | tf_op jit(solution)/shard_map/ppermute | solution.py:275
  171.3 53.9 %collective-permute-start.2 = (f32[2,128,2048]{2,1,0:T(8,128)}, f32[2,128,2048]{2,1,0:T(8,128)}, u32[]{:S(2)}, u32[]{:S(2)}) collective-permute-start(f32[2,128,2048]{2,1,0:T(8,128)} %get-tuple-element.54), channel_id=1, source_target_pairs={{0,1},{1,2},{2,3},{3,4},{4,5},{5,6},{6,7},{7,8},{8,9},{9,10},{10,1... | collective-permute-start | bytes 6291464 | tf_op jit(solution)/shard_map/ppermute | solution.py:274
  206.5 0.8 copy-start.8
  213.2 0.8 copy-start.7
  223.0 2.1 copy-start.5
  225.2 2.9 %copy-start.10 = (bf16[256,1024]{1,0:T(8,128)(2,1)S(1)}, bf16[256,1024]{1,0:T(8,128)(2,1)}, u32[]{:S(2)}) copy-start(bf16[256,1024]{1,0:T(8,128)(2,1)} %reshape.256) | copy-start | bytes 1572868
  225.2 49.5 %slice-start.1 = ((s8[6291456]{0:T(1024)(128)(4,1)}), s8[2097152]{0:T(1024)(128)(4,1)S(1)}, s32[]{:S(2)}) async-start(s8[6291456]{0:T(1024)(128)(4,1)} %bitcast.131), calls=%async_computation.1 | async-start | bytes 4194304
  228.0 1.0 copy-start.2
  229.1 45.6 %slice-start.2 = ((s8[6291456]{0:T(1024)(128)(4,1)}), s8[4194304]{0:T(1024)(128)(4,1)S(1)}, s32[]{:S(2)}) async-start(s8[6291456]{0:T(1024)(128)(4,1)} %bitcast.131), calls=%async_computation.2 | async-start | bytes 8388608
  271.3 3.4 %copy-start.4 = (bf16[2,128,1024]{2,1,0:T(8,128)(2,1)S(1)}, bf16[2,128,1024]{2,1,0:T(8,128)(2,1)}, u32[]{:S(2)}) copy-start(bf16[2,128,1024]{2,1,0:T(8,128)(2,1)} %param.16) | copy-start | bytes 1572868
  271.3 3.4 %copy-start.11 = (bf16[2,128,1024]{2,1,0:T(8,128)(2,1)S(1)}, bf16[2,128,1024]{2,1,0:T(8,128)(2,1)}, u32[]{:S(2)}) copy-start(bf16[2,128,1024]{2,1,0:T(8,128)(2,1)} %copy.70) | copy-start | bytes 1572868
  274.8 2.2 copy-start.6

commit v2 on v0

v2 whole, which is shorter than its diff:
```python
from types import SimpleNamespace

import jax
import jax.numpy as jnp
from jax import lax
from jax.experimental import pallas as pl
from jax.experimental.pallas import tpu as pltpu
from jax.sharding import PartitionSpec as P

RING = 4
MEMBERS_DEV = 2
ROWS = 256
WIDTH = 1024
HALF = 512
GROUP = 256
CHANNEL_GROUP = 16
LOG2E = 1.4426950408889634
F32 = jnp.float32
BF16 = jnp.bfloat16
MESH = pl.DeviceIdType.MESH

ORDERS = (("x", "y", "z"), ("y", "z", "x"), ("z", "x", "y"))
WIDTHS = ((384, 384, 384), (384, 384, 256))


class Place:
    def __init__(self):
        self.member = lax.axis_index("member")
        self.space = lax.axis_index("space")
        self.core = self.space % 2
        z_lo = (self.space // 2) % 2
        z_hi = self.member % 2
        self.at = {"x": self.space // 4, "y": self.member // 2, "z": z_hi * 2 + z_lo}

    def partner(self, axis, index):
        if axis == "x":
            return (self.member, index * 4 + self.space % 4)
        if axis == "y":
            return (index * 2 + self.member % 2, self.space)
        member = (self.member // 2) * 2 + index // 2
        return (member, (self.space // 4) * 4 + (index % 2) * 2 + self.core)

    def pair(self):
        return (self.member, self.space + 1 - 2 * self.core)

    def right(self):
        return (self.member, (self.space + 1) % 16)

    def left(self):
        return (self.member, (self.space + 15) % 16)

    def across(self, axis, offset):
        member, space = self.partner(axis, self.ahead(axis, offset))
        return (member, space + 1 - 2 * self.core)

    def ahead(self, axis, offset):
        return (self.at[axis] + offset) % RING


def chunk_order(order):
    where = []
    for y in range(4):
        for z_hi in range(2):
            for x in range(4):
                for z_lo in range(2):
                    digit = {"x": x, "y": y, "z": z_hi * 2 + z_lo}
                    a, b, c = (digit[name] for name in order)
                    where.append(a * 16 + b * 4 + c)
    return where


def remote(src, dst, send, recv, device):
    return pltpu.make_async_remote_copy(
        src_ref=src, dst_ref=dst, send_sem=send, recv_sem=recv, device_id=device, device_id_type=MESH
    )


def dot(a, b):
    return jnp.dot(a, b, preferred_element_type=F32)


def dot_nt(a, b):
    return lax.dot_general(a, b, (((1,), (1,)), ((), ())), preferred_element_type=F32)


def sign_of(a, b):
    one = jnp.float32(1.0)
    zero = jnp.float32(0.0)
    return jnp.where(a > b, one, zero) - jnp.where(a < b, one, zero)


def scratch():
    vmem = pltpu.VMEM
    dma = pltpu.SemaphoreType.DMA
    block3 = vmem((3, ROWS, WIDTH), BF16)
    rows_b = vmem((ROWS, WIDTH), BF16)
    rows_f = vmem((ROWS, WIDTH), F32)
    factor = vmem((2 * ROWS, HALF), BF16)
    turned = vmem((WIDTH, 2 * ROWS), BF16)

    def waves(*shape, dtype):
        return [[vmem((*shape, w), dtype) for w in widths] for widths in WIDTHS]

    return dict(
        w_in=vmem((WIDTH, 3 * WIDTH), BF16),
        w_back=vmem((WIDTH, WIDTH), BF16),
        w_dec=vmem((128, WIDTH), BF16),
        lat=block3, xn=block3, qx=block3, kx=block3, vx=block3, dx=block3,
        norm=rows_f, daf=rows_f, dk_acc=rows_f, dv_acc=rows_f, dnorm=rows_f,
        rstd=vmem((ROWS, 128), F32),
        daf_b=block3,
        att=rows_b, att_o=rows_b,
        dqkv=vmem((ROWS, 3 * WIDTH), BF16),
        mask=vmem((4 * 128, GROUP), BF16),
        stat=vmem((4, 8, 512), F32),
        stat_n=vmem((2, 4, 8, 512), F32),
        pred_p=vmem((2, 128, 128), F32),
        targ_p=vmem((128, 128), F32),
        pred_g=vmem((8, 2, CHANNEL_GROUP, 128), F32),
        crps_g=vmem((8, 2, CHANNEL_GROUP, 128), BF16),
        cr=vmem((3, 2, 128, 128), BF16),
        cr_rows=vmem((ROWS, 128), BF16),
        d_q=factor, d_k=factor, d_v=factor, d_o=factor,
        xt=[turned] * 3,
        at=[turned] * 2,
        ft=vmem((WIDTH, ROWS), BF16),
        send1=waves(6, 128, dtype=BF16),
        recv1=waves(6, 128, dtype=BF16),
        hold=waves(2, 128, dtype=F32),
        acc1=waves(256, dtype=F32),
        send2=waves(3, 64, dtype=BF16),
        recv2=waves(3, 64, dtype=BF16),
        acc2=waves(64, dtype=F32),
        recv3=waves(7, 8, dtype=F32),
        load=dma((5,)),
        halo_s=dma((2,)), halo_r=dma((2,)),
        pred_s=dma((7,)), pred_r=dma((7,)),
        back_s=dma((7,)), back_r=dma((7,)),
        crh_s=dma((2,)), crh_r=dma((2,)),
        sth_s=dma((2,)), sth_r=dma((2,)),
        pair_s=dma((5,)), pair_r=dma((5,)),
        ring_s=dma((96,)), ring_r=dma((96,)),
    )


SHAPES, TREE = jax.tree.flatten(scratch())


def kernel(
    latent, predictions, target, area_weight, slab_count, w_qkv, w_o, w_out, g_latent, g_qkv, g_o, g_out, *buffers
):
    r = SimpleNamespace(**jax.tree.unflatten(TREE, buffers))
    place = Place()
    core, member, slab = place.core, place.member, place.space
    sent = []

    def start(copy):
        copy.start()
        sent.append(copy)
        return copy

    load = r.load
    loads = [
        pltpu.make_async_copy(latent, r.lat.at[1], load.at[0]),
        pltpu.make_async_copy(w_qkv.at[:, pl.ds(0, WIDTH)], r.w_in.at[:, pl.ds(0, WIDTH)], load.at[1]),
        pltpu.make_async_copy(w_qkv.at[:, pl.ds(WIDTH, WIDTH)], r.w_in.at[:, pl.ds(WIDTH, WIDTH)], load.at[2]),
        pltpu.make_async_copy(
            w_qkv.at[:, pl.ds(2 * WIDTH, WIDTH)], r.w_in.at[:, pl.ds(2 * WIDTH, WIDTH)], load.at[3]
        ),
        pltpu.make_async_copy(w_o, r.w_back, load.at[4]),
    ]
    for copy in loads:
        copy.start()

    barrier = pltpu.get_barrier_semaphore()
    greeted = [((member + o) % 8, slab) for o in range(1, 8)]
    greeted += [place.partner(axis, place.ahead(axis, o)) for axis in ("x", "z") for o in (1, 2, 3)]
    greeted += [place.right(), place.left()]
    greeted += [place.across(axis, o) for axis in ("x", "y", "z") for o in (1, 2, 3)]
    for device in greeted:
        pl.semaphore_signal(barrier, inc=1, device_id=device, device_id_type=MESH)

    r.pred_p[...] = jnp.zeros((2, 128, 128), F32)
    r.targ_p[...] = jnp.zeros((128, 128), F32)
    r.w_dec[...] = jnp.zeros((128, WIDTH), BF16)
    channels = target.shape[0]
    for m in range(MEMBERS_DEV):
        r.pred_p[m, :channels, :] = predictions[:, m, :]
    r.targ_p[:channels, :] = target[...]
    r.w_dec[:channels, :] = w_out[...]
    head_row = lax.broadcasted_iota(jnp.int32, (512, GROUP), 0) // 128
    head_col = lax.broadcasted_iota(jnp.int32, (512, GROUP), 1) // 64
    r.mask[...] = jnp.where(head_row == head_col, jnp.float32(1.0), jnp.float32(0.0)).astype(BF16)

    pl.semaphore_wait(barrier, len(greeted))

    pred_copies = []
    for o in range(1, 8):
        dest = (member + o) % 8
        pred_copies.append(start(remote(
            r.pred_p.at[:, pl.ds(pl.multiple_of(dest * CHANNEL_GROUP, CHANNEL_GROUP), CHANNEL_GROUP)],
            r.pred_g.at[member], r.pred_s.at[o - 1], r.pred_r.at[o - 1], (dest, slab),
        )))
    halo = [
        start(remote(latent, r.lat.at[0], r.halo_s.at[0], r.halo_r.at[0], place.right())),
        start(remote(latent, r.lat.at[2], r.halo_s.at[1], r.halo_r.at[1], place.left())),
    ]

    def normalise(block, keep):
        xf = r.lat[block].astype(F32)
        mean = jnp.mean(xf, axis=-1, keepdims=True)
        cent = xf - mean
        var = jnp.mean(cent * cent, axis=-1, keepdims=True)
        rstd = lax.rsqrt(var + 1e-05)
        norm = cent * rstd
        r.xn[block] = norm.astype(BF16)
        if keep:
            r.norm[...] = norm
            r.rstd[...] = jnp.broadcast_to(rstd, (ROWS, 128))

    def project(block):
        for j in range(6):
            piece = dot(r.xn[block], r.w_in[:, j * HALF : (j + 1) * HALF]).astype(BF16)
            at = slice((j % 2) * HALF, (j % 2 + 1) * HALF)
            if j < 2:
                r.qx[block, :, at] = piece * jnp.bfloat16(0.125)
            elif j < 4:
                r.kx[block, :, at] = piece
            else:
                r.vx[block, :, at] = piece

    loads[0].wait()
    normalise(1, True)
    for copy in loads[1:]:
        copy.wait()
    project(1)

    r.pred_g[member] = r.pred_p[:, pl.ds(pl.multiple_of(member * CHANNEL_GROUP, CHANNEL_GROUP), CHANNEL_GROUP), :]
    for copy in pred_copies:
        copy.wait_recv()
    y = [r.pred_g[i // 2, i % 2] for i in range(16)]
    pair_sum = [jnp.zeros((CHANNEL_GROUP, 128), F32) for _ in range(16)]
    for i in range(16):
        for k in range(i + 1, 16):
            s = sign_of(y[i], y[k])
            pair_sum[i] = pair_sum[i] + s
            pair_sum[k] = pair_sum[k] - s
    point = lax.broadcasted_iota(jnp.int32, (1, 128), 1)
    pweight = jnp.where(point < slab_count[0], area_weight[...], jnp.zeros((1, 128), F32))
    truth = r.targ_p[pl.ds(pl.multiple_of(member * CHANNEL_GROUP, CHANNEL_GROUP), CHANNEL_GROUP), :]
    for i in range(16):
        crps = pweight * (sign_of(y[i], truth) - pair_sum[i] / 15.0)
        r.crps_g[i // 2, i % 2] = crps.astype(BF16)
    own_group = pl.ds(pl.multiple_of(member * CHANNEL_GROUP, CHANNEL_GROUP), CHANNEL_GROUP)
    back_copies = []
    for o in range(1, 8):
        dest = (member + o) % 8
        back_copies.append(start(remote(
            r.crps_g.at[dest], r.cr.at[1, :, own_group], r.back_s.at[o - 1], r.back_r.at[o - 1], (dest, slab)
        )))
    r.cr[1, :, own_group, :] = r.crps_g[member]

    near, far = 2 - 2 * core, 2 * core
    near_i, far_i = 1 - core, core

    def arrived(src, dst, send, recv, side, i):
        remote(src, dst.at[side], send.at[i], recv.at[i], place.pair()).wait_recv()

    arrived(latent, r.lat, r.halo_s, r.halo_r, near, near_i)
    normalise(near, False)
    project(near)

    for copy in back_copies:
        copy.wait_recv()
    crh = [
        start(remote(r.cr.at[1], r.cr.at[0], r.crh_s.at[0], r.crh_r.at[0], place.right())),
        start(remote(r.cr.at[1], r.cr.at[2], r.crh_s.at[1], r.crh_r.at[1], place.left())),
    ]

    def decode(block):
        for m in range(2):
            turned = r.cr[block, m].T
            value = dot(turned, r.w_dec[...])
            at = slice(m * 128, m * 128 + 128)
            r.daf_b[block, at, :] = value.astype(BF16)
            if isinstance(block, int):
                r.daf[at, :] = value
                r.cr_rows[at, :] = turned

    def attend_back(block):
        for j in range(4):
            at = slice(j * GROUP, (j + 1) * GROUP)
            r.dx[block, :, at] = dot_nt(r.daf_b[block], r.w_back[at, :]).astype(BF16)

    def lay(value, targets, column):
        turned = value.T
        for ref, order in targets:
            for chunk, spot in enumerate(chunk_order(order)):
                ref[spot * 16 : spot * 16 + 16, column : column + ROWS] = turned[chunk * 16 : chunk * 16 + 16]

    xts = [(r.xt[0], ORDERS[0]), (r.xt[1], ORDERS[1]), (r.xt[2], ORDERS[2])]
    ats = [(r.at[0], ORDERS[1]), (r.at[1], ORDERS[2])]

    decode(1)
    theirs = pl.multiple_of((1 - core) * HALF, HALF)
    high_rows = pl.ds(ROWS, ROWS)

    def give(i, src, dst):
        return start(remote(src, dst, r.pair_s.at[i], r.pair_r.at[i], place.pair()))

    pair_o = give(0, r.daf_b.at[1, :, pl.ds(theirs, HALF)], r.d_o.at[high_rows])
    attend_back(1)
    arrived(r.cr.at[1], r.cr, r.crh_s, r.crh_r, near, near_i)
    decode(near)
    attend_back(near)
    lay(r.xn[1], xts, 0)
    lay(r.xn[near], xts, ROWS)
    arrived(r.cr.at[1], r.cr, r.crh_s, r.crh_r, far, far_i)
    decode(far)
    attend_back(far)
    arrived(latent, r.lat, r.halo_s, r.halo_r, far, far_i)
    normalise(far, False)
    project(far)

    edge = [
        jnp.where(slab > 0, jnp.float32(0.0), jnp.float32(-1e30)),
        jnp.where(slab < 15, jnp.float32(0.0), jnp.float32(-1e30)),
    ]

    def spread(block):
        return jnp.concatenate([block, block, block, block], axis=0) * r.mask[...]

    def gather_heads(value):
        return jnp.concatenate(
            [value[h * 64 : (h + 1) * 64, h * 128 : (h + 1) * 128] for h in range(4)], axis=0
        ).T

    def own_queries(g, carry):
        cols = pl.ds(pl.multiple_of(g * GROUP, GROUP), GROUP)
        for m in range(2):
            rows = slice(m * 128, (m + 1) * 128)
            keys = jnp.concatenate([r.kx[b, rows, cols] for b in range(3)], axis=0)
            values = jnp.concatenate([r.vx[b, rows, cols] for b in range(3)], axis=0)
            q_b = spread(r.qx[1, rows, cols])
            d_b = spread(r.dx[1, rows, cols])
            scores = dot_nt(keys, q_b)
            scores = jnp.concatenate([scores[:128] + edge[0], scores[128:256], scores[256:] + edge[1]], axis=0)
            top = jnp.max(scores, axis=0, keepdims=True) * LOG2E
            e = jnp.exp2(scores * LOG2E - top)
            total = jnp.sum(e, axis=0, keepdims=True)
            prob = e * (1.0 / total)
            prob_b = prob.astype(BF16)
            dprob = dot_nt(values, d_b)
            delta = jnp.sum(dprob * prob, axis=0, keepdims=True)
            dscore = (prob * (dprob - delta)).astype(BF16)
            r.att[rows, cols] = gather_heads(dot(values.T, prob_b)).astype(BF16)
            r.dqkv[rows, cols] = (gather_heads(dot(keys.T, dscore)) * 0.125).astype(BF16)
            r.dk_acc[rows, cols] = dot(dscore[128:256], q_b)
            r.dv_acc[rows, cols] = dot(prob_b[128:256], d_b)
            r.stat[g, 2 * m : 2 * m + 1, :] = top + jnp.log2(total)
            r.stat[g, 2 * m + 1 : 2 * m + 2, :] = delta
        return carry

    r.stat[...] = jnp.zeros((4, 8, 512), F32)
    lax.fori_loop(0, 4, own_queries, 0)
    sth = [
        start(remote(r.stat, r.stat_n.at[0], r.sth_s.at[0], r.sth_r.at[0], place.right())),
        start(remote(r.stat, r.stat_n.at[1], r.sth_s.at[1], r.sth_r.at[1], place.left())),
    ]
    pair_a = give(1, r.att, r.att_o)
    pair_q = give(2, r.dqkv.at[:, pl.ds(theirs, HALF)], r.d_q.at[high_rows])

    def mine(ref, at, begin):
        return jnp.where(core == 0, ref[at, begin : begin + HALF], ref[at, begin + HALF : begin + 2 * HALF])

    r.d_o[:ROWS] = mine(r.daf_b.at[1], slice(0, ROWS), 0)
    r.d_q[:ROWS] = mine(r.dqkv, slice(0, ROWS), 0)

    after = r.lat[1].astype(F32) + dot(r.att[...], r.w_back[...])
    lay(after.astype(BF16), [(r.ft, ORDERS[2])], 0)
    lay(r.att[...], ats, 0)
    pair_a.wait_recv()
    lay(r.att_o[...], ats, ROWS)

    def terms(wave, p, dest):
        at = pl.ds(pl.multiple_of(dest * 256, 256), 256)
        if wave == 0:
            if p == 0:
                return [dot(r.xt[0][at, :], r.d_q[:, :384])]
            if p == 1:
                return [dot(r.xt[1][at, :], r.d_q[:, 384:]), dot(r.at[0][at, :], r.d_o[:, :256])]
            return [dot(r.at[1][at, :], r.d_o[:, 256:]), dot(r.ft[at, :], r.cr_rows[...])]
        if p == 0:
            return [dot(r.xt[0][at, :], r.d_k[:, :384])]
        if p == 1:
            return [dot(r.xt[1][at, :], r.d_k[:, 384:]), dot(r.xt[1][at, :], r.d_v[:, :256])]
        return [dot(r.xt[2][at, :], r.d_v[:, 256:])]

    def push(wave, p, slot, src, dst, device):
        slot = (wave * 3 + p) * 16 + slot
        return start(remote(src, dst, r.ring_s.at[slot], r.ring_r.at[slot], device))

    def neighbour(p, phase, offset):
        axis = ORDERS[p][phase]
        return place.partner(axis, place.ahead(axis, offset))

    def put(ref, index, values, dtype, rows=slice(None)):
        begin = 0
        for value in values:
            end = begin + value.shape[1]
            ref[index, rows, begin:end] = value.astype(dtype)
            begin = end

    def first(wave):
        copies = {}

        def go(p, slot, offset):
            copies[p, slot] = push(
                wave, p, slot, r.send1[wave][p].at[slot], r.recv1[wave][p].at[slot], neighbour(p, 0, offset)
            )

        for p in range(3):
            values = terms(wave, p, place.ahead(ORDERS[p][0], 2))
            put(r.send1[wave][p], 0, [v[:128] for v in values], BF16)
            put(r.send1[wave][p], 1, [v[128:] for v in values], BF16)
            go(p, 0, 1)
            go(p, 1, 3)
        for p in range(3):
            values = terms(wave, p, place.ahead(ORDERS[p][0], 1))
            put(r.send1[wave][p], 2, [v[128:] for v in values], BF16)
            put(r.hold[wave][p], 0, [v[:128] for v in values], F32)
            go(p, 2, 1)
            values = terms(wave, p, place.ahead(ORDERS[p][0], 3))
            put(r.send1[wave][p], 3, [v[:128] for v in values], BF16)
            put(r.hold[wave][p], 1, [v[128:] for v in values], F32)
            go(p, 3, 3)
        return copies

    def relay(wave, copies):
        for p in range(3):
            for half, offset in ((0, 1), (1, 3)):
                copies[p, half].wait_recv()
                r.send1[wave][p][4 + half] = (r.hold[wave][p][half] + r.recv1[wave][p][half].astype(F32)).astype(BF16)
                copies[p, 4 + half] = push(
                    wave, p, 4 + half, r.send1[wave][p].at[4 + half], r.recv1[wave][p].at[4 + half],
                    neighbour(p, 0, offset),
                )

    def own_terms(wave):
        for p in range(3):
            begin = 0
            for value in terms(wave, p, place.at[ORDERS[p][0]]):
                end = begin + value.shape[1]
                r.acc1[wave][p][:, begin:end] = value
                begin = end

    def second(wave, arrivals):
        copies = {}
        for p in range(3):
            acc, came = r.acc1[wave][p], r.recv1[wave][p]
            for slot in (2, 3, 4, 5):
                arrivals[p, slot].wait_recv()
            acc[:128] += came[3].astype(F32) + came[4].astype(F32)
            acc[128:] += came[2].astype(F32) + came[5].astype(F32)
            for offset in (2, 1, 3):
                dest = place.ahead(ORDERS[p][1], offset)
                r.send2[wave][p][offset - 1] = acc[pl.ds(pl.multiple_of(dest * 64, 64), 64), :].astype(BF16)
                copies[p, offset] = push(
                    wave, p, 5 + offset, r.send2[wave][p].at[offset - 1], r.recv2[wave][p].at[offset - 1],
                    neighbour(p, 1, offset),
                )
        return copies

    def third(wave, arrivals):
        copies = []
        for p in range(3):
            for offset in (1, 2, 3):
                arrivals[p, offset].wait_recv()
            own = r.acc1[wave][p][pl.ds(pl.multiple_of(place.at[ORDERS[p][1]] * 64, 64), 64), :]
            came = r.recv2[wave][p]
            r.acc2[wave][p][...] = own + (came[0].astype(F32) + came[1].astype(F32) + came[2].astype(F32))
            for offset in (2, 1, 3, 0):
                dest = place.ahead(ORDERS[p][2], offset)
                device = neighbour(p, 2, offset)
                for other in ((0, 1) if offset else (1,)):
                    side = core if other == 0 else 1 - core
                    slot = 3 + offset if other else offset - 1
                    src = r.acc2[wave][p].at[pl.ds(pl.multiple_of(dest * 16 + side * 8, 8), 8)]
                    to = (device[0], device[1] + (side - core))
                    copies.append(push(wave, p, 9 + slot, src, r.recv3[wave][p].at[slot], to))
        return copies

    def finish(wave, arrivals):
        for copy in arrivals:
            copy.wait_recv()
        own, other = [], []
        for p in range(3):
            came = r.recv3[wave][p]
            at = pl.ds(pl.multiple_of(place.at[ORDERS[p][2]] * 16 + core * 8, 8), 8)
            own.append(r.acc2[wave][p][at, :] + came[0] + came[1] + came[2])
            other.append(came[3] + came[4] + came[5] + came[6])
        return own, other

    def place_both(out, begin, own, other):
        width = own.shape[1]
        out[:, begin : begin + width] = jnp.where(core == 0, own, other)
        out[:, begin + HALF : begin + HALF + width] = jnp.where(core == 0, other, own)

    pair_o.wait_recv()
    pair_q.wait_recv()
    arrive0 = first(0)
    own_terms(0)

    for copy in sth:
        copy.wait_recv()

    def other_queries(g, carry):
        cols = pl.ds(pl.multiple_of(g * GROUP, GROUP), GROUP)
        for m in range(2):
            rows = slice(m * 128, (m + 1) * 128)
            keys = r.kx[1, rows, cols]
            values = r.vx[1, rows, cols]
            dk = r.dk_acc[rows, cols]
            dv = r.dv_acc[rows, cols]
            for side in range(2):
                q_b = spread(r.qx[2 * side, rows, cols])
                d_b = spread(r.dx[2 * side, rows, cols])
                lse = r.stat_n[side, g, 2 * m : 2 * m + 1, :]
                delta = r.stat_n[side, g, 2 * m + 1 : 2 * m + 2, :]
                prob = jnp.exp2(dot_nt(keys, q_b) * LOG2E - (lse - edge[side]))
                dscore = (prob * (dot_nt(values, d_b) - delta)).astype(BF16)
                dk += dot(dscore, q_b)
                dv += dot(prob.astype(BF16), d_b)
            r.dqkv[rows, pl.ds(pl.multiple_of(WIDTH + g * GROUP, GROUP), GROUP)] = dk.astype(BF16)
            r.dqkv[rows, pl.ds(pl.multiple_of(2 * WIDTH + g * GROUP, GROUP), GROUP)] = dv.astype(BF16)
        return carry

    lax.fori_loop(0, 2, other_queries, 0)
    relay(0, arrive0)
    lax.fori_loop(2, 4, other_queries, 0)
    pair_k = give(3, r.dqkv.at[:, pl.ds(pl.multiple_of(WIDTH + theirs, HALF), HALF)], r.d_k.at[high_rows])
    pair_v = give(4, r.dqkv.at[:, pl.ds(pl.multiple_of(2 * WIDTH + theirs, HALF), HALF)], r.d_v.at[high_rows])
    r.d_k[:ROWS] = mine(r.dqkv, slice(0, ROWS), WIDTH)
    r.d_v[:ROWS] = mine(r.dqkv, slice(0, ROWS), 2 * WIDTH)
    arrive0 = second(0, arrive0)
    pair_k.wait_recv()
    pair_v.wait_recv()
    arrive1 = first(1)
    arrive0 = third(0, arrive0)
    own_terms(1)
    relay(1, arrive1)

    for j in range(4):
        at = slice(j * GROUP, (j + 1) * GROUP)
        r.dnorm[:, at] = dot_nt(r.dqkv[...], r.w_in[at, :])
    dnorm = r.dnorm[...]
    norm = r.norm[...]
    dlayer = r.rstd[:, :1] * (
        dnorm
        - jnp.mean(dnorm, axis=-1, keepdims=True)
        - norm * jnp.mean(dnorm * norm, axis=-1, keepdims=True)
    )
    g_latent[...] = (r.daf[...] + dlayer).astype(BF16)

    arrive1 = second(1, arrive1)
    own, other = finish(0, arrive0)
    place_both(g_qkv, 0, own[0], other[0])
    place_both(g_qkv, 384, own[1][:, :128], other[1][:, :128])
    place_both(g_o, 0, own[1][:, 128:], other[1][:, 128:])
    place_both(g_o, 256, own[2][:, :256], other[2][:, :256])
    total = own[2][:, 256:] + other[2][:, 256:]
    g_out[...] = total[:, :channels]

    arrive1 = third(1, arrive1)
    own, other = finish(1, arrive1)
    place_both(g_qkv, WIDTH, own[0], other[0])
    place_both(g_qkv, WIDTH + 384, own[1][:, :128], other[1][:, :128])
    place_both(g_qkv, 2 * WIDTH, own[1][:, 128:], other[1][:, 128:])
    place_both(g_qkv, 2 * WIDTH + 256, own[2], other[2])
    for copy in sent:
        copy.wait_send()


def hand_over(*refs):
    for source, target in zip(refs[:4], refs[4:]):
        target[...] = source[...]


def on_device(latent, predictions, target, area_weight, slab_count, w_qkv, w_o, w_out):
    members_here, points, width = latent.shape
    channels = predictions.shape[1]
    rows = members_here * points
    vmem = pl.BlockSpec(memory_space=pltpu.VMEM)
    hbm = pl.BlockSpec(memory_space=pl.ANY)
    smem = pl.BlockSpec(memory_space=pltpu.SMEM)
    shapes = (
        jax.ShapeDtypeStruct((rows, width), BF16),
        jax.ShapeDtypeStruct((8, 3 * width), F32),
        jax.ShapeDtypeStruct((8, width), F32),
        jax.ShapeDtypeStruct((8, channels), F32),
    )
    grad_latent, grad_qkv, grad_o, grad_out = pl.pallas_call(
        kernel,
        out_shape=shapes,
        in_specs=[hbm, vmem, vmem, vmem, smem, hbm, hbm, vmem],
        out_specs=[vmem] * 4,
        scratch_shapes=SHAPES,
        compiler_params=pltpu.CompilerParams(
            collective_id=0, has_side_effects=True, vmem_limit_bytes=62 * 1024 * 1024
        ),
    )(
        latent.reshape(rows, width), predictions.transpose(1, 0, 2), target, area_weight.reshape(1, points),
        slab_count, w_qkv, w_o, w_out.T,
    )
    grad_latent, grad_qkv, grad_o, grad_out = pl.pallas_call(
        hand_over,
        out_shape=shapes,
        in_specs=[vmem] * 4,
        out_specs=[vmem] * 4,
    )(grad_latent, grad_qkv, grad_o, grad_out)
    return grad_latent.reshape(latent.shape), grad_qkv, grad_o, grad_out


def solution(mesh):
    placed = (
        P("member", "space", None),
        P("member", None, "space"),
        P(None, "space"),
        P("space"),
        P("space"),
        P(),
        P(),
        P(),
    )
    return jax.shard_map(
        on_device,
        mesh=mesh,
        in_specs=placed,
        out_specs=(
            P("member", "space", None),
            P(("member", "space"), None),
            P(("member", "space"), None),
            P(("member", "space"), None),
        ),
        check_vma=False,
    )
```

time: 1580 us -> 79.9 us (0.05)
  waiting for transfers between devices: 1320 us -> 0 us
  matrix products: 108 us -> 0 us
  Pallas kernels: 0 us -> 78.4 us
  blocking collectives: 53.4 us -> 0 us
  local copies, waits for them, and re-layouts: 41 us -> 0 us
    reduce_scatter x2 -> x0, waiting for transfers between devices: 1290 us -> none  [the longest x1 654 us: on_device(): lax.psum_scatter(term_qkv, ('member', 'space'), scatter_dimension=0, tile...]
    dot_general x12 -> x0, matrix products: 102 us -> none  [the longest x1 32.1 us: on_device(): jnp.einsum('mnhqk,mnqhd->mnkhd', dscore, qh, preferred_element_type=jnp.f...]
    pallas_call x0 -> x2, Pallas kernels: none -> 78.4 us  [the longest x1 76.5 us: on_device(): pl.pallas_call(kernel, out_shape=shapes, in_specs=[hbm, vmem, vmem, vmem,...]
    all_gather x1 -> x0, blocking collectives: 53.4 us -> none  [on_device(): every = lax.all_gather(predictions, 'member', axis=0, tiled=True)]
    unnamed x4 -> x0, waiting for transfers between devices: 29.3 us -> none
    concatenate x4 -> x0, local copies, waits for them, and re-layouts: 21.5 us -> none  [on_device(): jnp.concatenate([dkey.reshape(members_here, nblk, 3 * BLOCK, width), dval...]
  transfers between devices with their start and end apart: 7 -> 0, of which waited for: 4 -> 0; matrix products, arithmetic and copies ran while one was open for 8% -> 0% of each run, Pallas kernels for 0% -> 0%
where the time goes in v2:
time: 79.9 us; the launch traced here: 79.7 us
  Pallas kernels  78.4 us (98%)
  between operations  1.29 us (2%)
    pallas_call x1, Pallas kernels, on_device(): pl.pallas_call(kernel, out_shape=shapes, in_specs=[hbm, vmem, vmem, vmem,...  76.5 us
    pallas_call x1, Pallas kernels, on_device(): pl.pallas_call(hand_over, out_shape=shapes, in_specs=[vmem] * 4, out_spec...  1.94 us

profile of v2, /device:TPU:1, one launch (start us, length us, event | category | flops | bytes accessed | tf_op | source)
XLA Modules:
  0.0 79.7 jit_solution(1301171660853165548)
XLA Ops:
  1.3 76.5 %shard_map.111 = (bf16[256,1024]{1,0:T(8,128)(2,1)}, f32[8,3072]{1,0:T(8,128)}, f32[8,1024]{1,0:T(8,128)}, f32[8,100]{1,0:T(8,128)}) custom-call(bf16[256,1024]{1,0:T(8,128)(2,1)} %bitcast.5, f32[100,2,128]{2,1,0:T(2,128)} %bitcast.7, f32[100,128]{1,0:T(8,128)} %target.1, f32[1,128]{1,0:T(1,128)} %bitcast.8, s32[1]{0:T(128)S(6)} %copy.12.slab_count, ...), custom_call_target="tpu_custom_call" | custom-call | tf_op jit(solution)/shard_map/pallas_call | solution.py:602
  77.8 1.9 %shard_map.112 = (bf16[256,1024]{1,0:T(8,128)(2,1)}, f32[8,3072]{1,0:T(8,128)}, f32[8,1024]{1,0:T(8,128)}, f32[8,100]{1,0:T(8,128)}) custom-call(bf16[256,1024]{1,0:T(8,128)(2,1)} %get-tuple-element.12.refs_0_, f32[8,3072]{1,0:T(8,128)} %get-tuple-element.13.refs_1_, f32[8,1024]{1,0:T(8,128)} %get-tuple-element.14.refs_2_, f32[8,100]{1,0:T(8,128)} %get-tuple-element.15.refs_3_), custom_call_target="tpu_custom_call" | custom-call | tf_op jit(solution)/shard_map/pallas_call | solution.py:615

commit v3 on v2

--- a/solution.py
+++ b/solution.py
@@ -112,8 +112,8 @@
         att=rows_b, att_o=rows_b,
         dqkv=vmem((ROWS, 3 * WIDTH), BF16),
         mask=vmem((4 * 128, GROUP), BF16),
-        stat=vmem((4, 8, 512), F32),
-        stat_n=vmem((2, 4, 8, 512), F32),
+        stat=vmem((2, 2, 8, 512), F32),
+        stat_n=vmem((2, 2, 2, 8, 512), F32),
         pred_p=vmem((2, 128, 128), F32),
         targ_p=vmem((128, 128), F32),
         pred_g=vmem((8, 2, CHANNEL_GROUP, 128), F32),
@@ -133,12 +133,12 @@
         acc2=waves(64, dtype=F32),
         recv3=waves(7, 8, dtype=F32),
         load=dma((5,)),
-        halo_s=dma((2,)), halo_r=dma((2,)),
+        halo_s=dma((3,)), halo_r=dma((3,)),
         pred_s=dma((7,)), pred_r=dma((7,)),
         back_s=dma((7,)), back_r=dma((7,)),
         crh_s=dma((2,)), crh_r=dma((2,)),
-        sth_s=dma((2,)), sth_r=dma((2,)),
-        pair_s=dma((5,)), pair_r=dma((5,)),
+        sth_s=dma((4,)), sth_r=dma((4,)),
+        pair_s=dma((6,)), pair_r=dma((6,)),
         ring_s=dma((96,)), ring_r=dma((96,)),
     )
 
@@ -180,17 +180,10 @@
     for device in greeted:
         pl.semaphore_signal(barrier, inc=1, device_id=device, device_id_type=MESH)
 
-    r.pred_p[...] = jnp.zeros((2, 128, 128), F32)
-    r.targ_p[...] = jnp.zeros((128, 128), F32)
-    r.w_dec[...] = jnp.zeros((128, WIDTH), BF16)
+    r.pred_p[:, 96:, :] = jnp.zeros((2, 32, 128), F32)
     channels = target.shape[0]
     for m in range(MEMBERS_DEV):
         r.pred_p[m, :channels, :] = predictions[:, m, :]
-    r.targ_p[:channels, :] = target[...]
-    r.w_dec[:channels, :] = w_out[...]
-    head_row = lax.broadcasted_iota(jnp.int32, (512, GROUP), 0) // 128
-    head_col = lax.broadcasted_iota(jnp.int32, (512, GROUP), 1) // 64
-    r.mask[...] = jnp.where(head_row == head_col, jnp.float32(1.0), jnp.float32(0.0)).astype(BF16)
 
     pl.semaphore_wait(barrier, len(greeted))
 
@@ -201,39 +194,56 @@
             r.pred_p.at[:, pl.ds(pl.multiple_of(dest * CHANNEL_GROUP, CHANNEL_GROUP), CHANNEL_GROUP)],
             r.pred_g.at[member], r.pred_s.at[o - 1], r.pred_r.at[o - 1], (dest, slab),
         )))
-    halo = [
-        start(remote(latent, r.lat.at[0], r.halo_s.at[0], r.halo_r.at[0], place.right())),
-        start(remote(latent, r.lat.at[2], r.halo_s.at[1], r.halo_r.at[1], place.left())),
-    ]
-
-    def normalise(block, keep):
-        xf = r.lat[block].astype(F32)
+    near, far = 2 - 2 * core, 2 * core
+    far_device = (member, (slab + 15 + 2 * core) % 16)
+    halo_near = start(remote(latent, r.lat.at[far], r.halo_s.at[0], r.halo_r.at[0], place.pair()))
+
+    def halo_part(i):
+        rows = pl.ds(i * 128, 128)
+        return start(remote(
+            latent.at[rows], r.lat.at[near, rows], r.halo_s.at[1 + i], r.halo_r.at[1 + i], far_device
+        ))
+
+    halo_far = [halo_part(0)]
+
+    r.targ_p[...] = jnp.zeros((128, 128), F32)
+    r.w_dec[...] = jnp.zeros((128, WIDTH), BF16)
+    r.targ_p[:channels, :] = target[...]
+    r.w_dec[:channels, :] = w_out[...]
+    head_row = lax.broadcasted_iota(jnp.int32, (512, GROUP), 0) // 128
+    head_col = lax.broadcasted_iota(jnp.int32, (512, GROUP), 1) // 64
+    r.mask[...] = jnp.where(head_row == head_col, jnp.float32(1.0), jnp.float32(0.0)).astype(BF16)
+
+    every = slice(0, ROWS)
+
+    def normalise(block, keep, rows=every):
+        xf = r.lat[block, rows, :].astype(F32)
         mean = jnp.mean(xf, axis=-1, keepdims=True)
         cent = xf - mean
         var = jnp.mean(cent * cent, axis=-1, keepdims=True)
         rstd = lax.rsqrt(var + 1e-05)
         norm = cent * rstd
-        r.xn[block] = norm.astype(BF16)
+        r.xn[block, rows, :] = norm.astype(BF16)
         if keep:
             r.norm[...] = norm
             r.rstd[...] = jnp.broadcast_to(rstd, (ROWS, 128))
 
-    def project(block):
-        for j in range(6):
-            piece = dot(r.xn[block], r.w_in[:, j * HALF : (j + 1) * HALF]).astype(BF16)
+    def project(block, begin, end, rows=every):
+        for j in range(begin, end):
+            piece = dot(r.xn[block, rows, :], r.w_in[:, j * HALF : (j + 1) * HALF]).astype(BF16)
             at = slice((j % 2) * HALF, (j % 2 + 1) * HALF)
             if j < 2:
-                r.qx[block, :, at] = piece * jnp.bfloat16(0.125)
+                r.qx[block, rows, at] = piece * jnp.bfloat16(0.125)
             elif j < 4:
-                r.kx[block, :, at] = piece
+                r.kx[block, rows, at] = piece
             else:
-                r.vx[block, :, at] = piece
+                r.vx[block, rows, at] = piece
 
     loads[0].wait()
     normalise(1, True)
     for copy in loads[1:]:
         copy.wait()
-    project(1)
+    project(1, 0, 6)
 
     r.pred_g[member] = r.pred_p[:, pl.ds(pl.multiple_of(member * CHANNEL_GROUP, CHANNEL_GROUP), CHANNEL_GROUP), :]
     for copy in pred_copies:
@@ -260,22 +270,7 @@
         )))
     r.cr[1, :, own_group, :] = r.crps_g[member]
 
-    near, far = 2 - 2 * core, 2 * core
-    near_i, far_i = 1 - core, core
-
-    def arrived(src, dst, send, recv, side, i):
-        remote(src, dst.at[side], send.at[i], recv.at[i], place.pair()).wait_recv()
-
-    arrived(latent, r.lat, r.halo_s, r.halo_r, near, near_i)
-    normalise(near, False)
-    project(near)
-
-    for copy in back_copies:
-        copy.wait_recv()
-    crh = [
-        start(remote(r.cr.at[1], r.cr.at[0], r.crh_s.at[0], r.crh_r.at[0], place.right())),
-        start(remote(r.cr.at[1], r.cr.at[2], r.crh_s.at[1], r.crh_r.at[1], place.left())),
-    ]
+    halo_far.append(halo_part(1))
 
     def decode(block):
         for m in range(2):
@@ -300,27 +295,28 @@
 
     xts = [(r.xt[0], ORDERS[0]), (r.xt[1], ORDERS[1]), (r.xt[2], ORDERS[2])]
     ats = [(r.at[0], ORDERS[1]), (r.at[1], ORDERS[2])]
-
-    decode(1)
     theirs = pl.multiple_of((1 - core) * HALF, HALF)
     high_rows = pl.ds(ROWS, ROWS)
 
     def give(i, src, dst):
         return start(remote(src, dst, r.pair_s.at[i], r.pair_r.at[i], place.pair()))
 
+    halo_near.wait_recv()
+    normalise(near, False)
+    project(near, 0, 6)
+    lay(r.xn[1], xts, 0)
+    lay(r.xn[near], xts, ROWS)
+    halo_far[0].wait_recv()
+    member_rows = [slice(0, 128), slice(128, 256)]
+    normalise(far, False, member_rows[0])
+    project(far, 2, 6, member_rows[0])
+    for copy in back_copies:
+        copy.wait_recv()
+    crh_near = start(remote(r.cr.at[1], r.cr.at[far], r.crh_s.at[0], r.crh_r.at[0], place.pair()))
+    crh_far = start(remote(r.cr.at[1], r.cr.at[near], r.crh_s.at[1], r.crh_r.at[1], far_device))
+    decode(1)
     pair_o = give(0, r.daf_b.at[1, :, pl.ds(theirs, HALF)], r.d_o.at[high_rows])
     attend_back(1)
-    arrived(r.cr.at[1], r.cr, r.crh_s, r.crh_r, near, near_i)
-    decode(near)
-    attend_back(near)
-    lay(r.xn[1], xts, 0)
-    lay(r.xn[near], xts, ROWS)
-    arrived(r.cr.at[1], r.cr, r.crh_s, r.crh_r, far, far_i)
-    decode(far)
-    attend_back(far)
-    arrived(latent, r.lat, r.halo_s, r.halo_r, far, far_i)
-    normalise(far, False)
-    project(far)
 
     edge = [
         jnp.where(slab > 0, jnp.float32(0.0), jnp.float32(-1e30)),
@@ -330,15 +326,18 @@
     def spread(block):
         return jnp.concatenate([block, block, block, block], axis=0) * r.mask[...]
 
-    def gather_heads(value):
+    def per_head(left, right):
         return jnp.concatenate(
-            [value[h * 64 : (h + 1) * 64, h * 128 : (h + 1) * 128] for h in range(4)], axis=0
+            [dot(left[h * 64 : (h + 1) * 64], right[:, h * 128 : (h + 1) * 128]) for h in range(4)], axis=0
         ).T
 
-    def own_queries(g, carry):
-        cols = pl.ds(pl.multiple_of(g * GROUP, GROUP), GROUP)
-        for m in range(2):
-            rows = slice(m * 128, (m + 1) * 128)
+    def group_cols(half, u, begin=0):
+        return pl.ds(pl.multiple_of(begin + half * HALF + u * GROUP, GROUP), GROUP)
+
+    def own_queries(m, half):
+        rows = member_rows[m]
+        for u in range(2):
+            cols = group_cols(half, u)
             keys = jnp.concatenate([r.kx[b, rows, cols] for b in range(3)], axis=0)
             values = jnp.concatenate([r.vx[b, rows, cols] for b in range(3)], axis=0)
             q_b = spread(r.qx[1, rows, cols])
@@ -353,22 +352,37 @@
             dprob = dot_nt(values, d_b)
             delta = jnp.sum(dprob * prob, axis=0, keepdims=True)
             dscore = (prob * (dprob - delta)).astype(BF16)
-            r.att[rows, cols] = gather_heads(dot(values.T, prob_b)).astype(BF16)
-            r.dqkv[rows, cols] = (gather_heads(dot(keys.T, dscore)) * 0.125).astype(BF16)
+            r.att[rows, cols] = per_head(values.T, prob_b).astype(BF16)
+            r.dqkv[rows, cols] = (per_head(keys.T, dscore) * 0.125).astype(BF16)
             r.dk_acc[rows, cols] = dot(dscore[128:256], q_b)
             r.dv_acc[rows, cols] = dot(prob_b[128:256], d_b)
-            r.stat[g, 2 * m : 2 * m + 1, :] = top + jnp.log2(total)
-            r.stat[g, 2 * m + 1 : 2 * m + 2, :] = delta
-        return carry
-
-    r.stat[...] = jnp.zeros((4, 8, 512), F32)
-    lax.fori_loop(0, 4, own_queries, 0)
-    sth = [
-        start(remote(r.stat, r.stat_n.at[0], r.sth_s.at[0], r.sth_r.at[0], place.right())),
-        start(remote(r.stat, r.stat_n.at[1], r.sth_s.at[1], r.sth_r.at[1], place.left())),
-    ]
-    pair_a = give(1, r.att, r.att_o)
-    pair_q = give(2, r.dqkv.at[:, pl.ds(theirs, HALF)], r.d_q.at[high_rows])
+            r.stat[m, half, 2 * u : 2 * u + 1, :] = top + jnp.log2(total)
+            r.stat[m, half, 2 * u + 1 : 2 * u + 2, :] = delta
+
+    def send_stat(m):
+        return [
+            start(remote(
+                r.stat.at[m], r.stat_n.at[core, m], r.sth_s.at[2 * m], r.sth_r.at[2 * m], place.pair()
+            )),
+            start(remote(
+                r.stat.at[m], r.stat_n.at[1 - core, m], r.sth_s.at[2 * m + 1], r.sth_r.at[2 * m + 1], far_device
+            )),
+        ]
+
+    r.stat[...] = jnp.zeros((2, 2, 8, 512), F32)
+    own_queries(0, 1 - core)
+    own_queries(0, core)
+    sth = send_stat(0)
+    halo_far[1].wait_recv()
+    normalise(far, False, member_rows[1])
+    project(far, 2, 6, member_rows[1])
+    own_queries(1, 1 - core)
+    own_half = pl.multiple_of(core * HALF, HALF)
+    pair_q = give(1, r.dqkv.at[:, pl.ds(theirs, HALF)], r.d_q.at[high_rows])
+    pair_a = [give(2, r.att.at[:, pl.ds(theirs, HALF)], r.att_o.at[:, pl.ds(theirs, HALF)])]
+    own_queries(1, core)
+    sth += send_stat(1)
+    pair_a.append(give(3, r.att.at[:, pl.ds(own_half, HALF)], r.att_o.at[:, pl.ds(own_half, HALF)]))
 
     def mine(ref, at, begin):
         return jnp.where(core == 0, ref[at, begin : begin + HALF], ref[at, begin + HALF : begin + 2 * HALF])
@@ -379,7 +393,8 @@
     after = r.lat[1].astype(F32) + dot(r.att[...], r.w_back[...])
     lay(after.astype(BF16), [(r.ft, ORDERS[2])], 0)
     lay(r.att[...], ats, 0)
-    pair_a.wait_recv()
+    for copy in pair_a:
+        copy.wait_recv()
     lay(r.att_o[...], ats, ROWS)
 
     def terms(wave, p, dest):
@@ -511,48 +526,53 @@
     arrive0 = first(0)
     own_terms(0)
 
+    for side, copy in ((near, crh_near), (far, crh_far)):
+        copy.wait_recv()
+        decode(side)
+        attend_back(side)
+    project(far, 0, 2)
+
+    def other_queries(half):
+        for m in range(2):
+            rows = member_rows[m]
+            for u in range(2):
+                cols = group_cols(half, u)
+                keys = r.kx[1, rows, cols]
+                values = r.vx[1, rows, cols]
+                dk = r.dk_acc[rows, cols]
+                dv = r.dv_acc[rows, cols]
+                for side in range(2):
+                    q_b = spread(r.qx[2 * side, rows, cols])
+                    d_b = spread(r.dx[2 * side, rows, cols])
+                    lse = r.stat_n[side, m, half, 2 * u : 2 * u + 1, :]
+                    delta = r.stat_n[side, m, half, 2 * u + 1 : 2 * u + 2, :]
+                    prob = jnp.exp2(dot_nt(keys, q_b) * LOG2E - (lse - edge[side]))
+                    dscore = (prob * (dot_nt(values, d_b) - delta)).astype(BF16)
+                    dk += dot(dscore, q_b)
+                    dv += dot(prob.astype(BF16), d_b)
+                r.dqkv[rows, group_cols(half, u, WIDTH)] = dk.astype(BF16)
+                r.dqkv[rows, group_cols(half, u, 2 * WIDTH)] = dv.astype(BF16)
+
     for copy in sth:
         copy.wait_recv()
-
-    def other_queries(g, carry):
-        cols = pl.ds(pl.multiple_of(g * GROUP, GROUP), GROUP)
-        for m in range(2):
-            rows = slice(m * 128, (m + 1) * 128)
-            keys = r.kx[1, rows, cols]
-            values = r.vx[1, rows, cols]
-            dk = r.dk_acc[rows, cols]
-            dv = r.dv_acc[rows, cols]
-            for side in range(2):
-                q_b = spread(r.qx[2 * side, rows, cols])
-                d_b = spread(r.dx[2 * side, rows, cols])
-                lse = r.stat_n[side, g, 2 * m : 2 * m + 1, :]
-                delta = r.stat_n[side, g, 2 * m + 1 : 2 * m + 2, :]
-                prob = jnp.exp2(dot_nt(keys, q_b) * LOG2E - (lse - edge[side]))
-                dscore = (prob * (dot_nt(values, d_b) - delta)).astype(BF16)
-                dk += dot(dscore, q_b)
-                dv += dot(prob.astype(BF16), d_b)
-            r.dqkv[rows, pl.ds(pl.multiple_of(WIDTH + g * GROUP, GROUP), GROUP)] = dk.astype(BF16)
-            r.dqkv[rows, pl.ds(pl.multiple_of(2 * WIDTH + g * GROUP, GROUP), GROUP)] = dv.astype(BF16)
-        return carry
-
-    lax.fori_loop(0, 2, other_queries, 0)
+    other_queries(1 - core)
+    pair_k = give(4, r.dqkv.at[:, pl.ds(pl.multiple_of(WIDTH + theirs, HALF), HALF)], r.d_k.at[high_rows])
+    pair_v = give(5, r.dqkv.at[:, pl.ds(pl.multiple_of(2 * WIDTH + theirs, HALF), HALF)], r.d_v.at[high_rows])
     relay(0, arrive0)
-    lax.fori_loop(2, 4, other_queries, 0)
-    pair_k = give(3, r.dqkv.at[:, pl.ds(pl.multiple_of(WIDTH + theirs, HALF), HALF)], r.d_k.at[high_rows])
-    pair_v = give(4, r.dqkv.at[:, pl.ds(pl.multiple_of(2 * WIDTH + theirs, HALF), HALF)], r.d_v.at[high_rows])
+    other_queries(core)
     r.d_k[:ROWS] = mine(r.dqkv, slice(0, ROWS), WIDTH)
     r.d_v[:ROWS] = mine(r.dqkv, slice(0, ROWS), 2 * WIDTH)
-    arrive0 = second(0, arrive0)
     pair_k.wait_recv()
     pair_v.wait_recv()
     arrive1 = first(1)
-    arrive0 = third(0, arrive0)
+    arrive0 = second(0, arrive0)
     own_terms(1)
-    relay(1, arrive1)
 
     for j in range(4):
         at = slice(j * GROUP, (j + 1) * GROUP)
         r.dnorm[:, at] = dot_nt(r.dqkv[...], r.w_in[at, :])
+    relay(1, arrive1)
+    arrive0 = third(0, arrive0)
     dnorm = r.dnorm[...]
     norm = r.norm[...]
     dlayer = r.rstd[:, :1] * (

time: 79.9 us -> 71.4 us (0.89)
  Pallas kernels: 78.4 us -> 69.9 us
    pallas_call x1, Pallas kernels: 76.5 us -> 68 us  [on_device(): pl.pallas_call(kernel, out_shape=shapes, in_specs=[hbm, vmem, vmem, vmem,...]
where the time goes in v3:
time: 71.4 us; the launch traced here: 71.2 us
  Pallas kernels  69.9 us (98%)
  between operations  1.29 us (2%)
    pallas_call x1, Pallas kernels, on_device(): pl.pallas_call(kernel, out_shape=shapes, in_specs=[hbm, vmem, vmem, vmem,...  68 us
    pallas_call x1, Pallas kernels, on_device(): pl.pallas_call(hand_over, out_shape=shapes, in_specs=[vmem] * 4, out_spec...  1.94 us

profile of v3, /device:TPU:1, one launch (start us, length us, event | category | flops | bytes accessed | tf_op | source)
XLA Modules:
  0.0 71.2 jit_solution(12437627299320223252)
XLA Ops:
  1.3 68.0 %shard_map.111 = (bf16[256,1024]{1,0:T(8,128)(2,1)}, f32[8,3072]{1,0:T(8,128)}, f32[8,1024]{1,0:T(8,128)}, f32[8,100]{1,0:T(8,128)}) custom-call(bf16[256,1024]{1,0:T(8,128)(2,1)} %bitcast.5, f32[100,2,128]{2,1,0:T(2,128)} %bitcast.7, f32[100,128]{1,0:T(8,128)} %target.1, f32[1,128]{1,0:T(1,128)} %bitcast.8, s32[1]{0:T(128)S(6)} %copy.12.slab_count, ...), custom_call_target="tpu_custom_call" | custom-call | tf_op jit(solution)/shard_map/pallas_call | solution.py:622
  69.3 1.9 %shard_map.112 = (bf16[256,1024]{1,0:T(8,128)(2,1)}, f32[8,3072]{1,0:T(8,128)}, f32[8,1024]{1,0:T(8,128)}, f32[8,100]{1,0:T(8,128)}) custom-call(bf16[256,1024]{1,0:T(8,128)(2,1)} %get-tuple-element.12.refs_0_, f32[8,3072]{1,0:T(8,128)} %get-tuple-element.13.refs_1_, f32[8,1024]{1,0:T(8,128)} %get-tuple-element.14.refs_2_, f32[8,100]{1,0:T(8,128)} %get-tuple-element.15.refs_3_), custom_call_target="tpu_custom_call" | custom-call | tf_op jit(solution)/shard_map/pallas_call | solution.py:635

commit v4 on v3

--- a/solution.py
+++ b/solution.py
@@ -111,7 +111,11 @@
         daf_b=block3,
         att=rows_b, att_o=rows_b,
         dqkv=vmem((ROWS, 3 * WIDTH), BF16),
-        mask=vmem((4 * 128, GROUP), BF16),
+        mask=vmem((2, 128, 128), BF16),
+        pred_in=vmem((200, 128), F32),
+        targ_in=vmem((100, 128), F32),
+        w_out_in=vmem((100, WIDTH), BF16),
+        g_stage=vmem((ROWS, WIDTH), BF16),
         stat=vmem((2, 2, 8, 512), F32),
         stat_n=vmem((2, 2, 2, 8, 512), F32),
         pred_p=vmem((2, 128, 128), F32),
@@ -132,7 +136,7 @@
         recv2=waves(3, 64, dtype=BF16),
         acc2=waves(64, dtype=F32),
         recv3=waves(7, 8, dtype=F32),
-        load=dma((5,)),
+        load=dma((9,)),
         halo_s=dma((3,)), halo_r=dma((3,)),
         pred_s=dma((7,)), pred_r=dma((7,)),
         back_s=dma((7,)), back_r=dma((7,)),
@@ -160,15 +164,12 @@
         return copy
 
     load = r.load
-    loads = [
-        pltpu.make_async_copy(latent, r.lat.at[1], load.at[0]),
-        pltpu.make_async_copy(w_qkv.at[:, pl.ds(0, WIDTH)], r.w_in.at[:, pl.ds(0, WIDTH)], load.at[1]),
-        pltpu.make_async_copy(w_qkv.at[:, pl.ds(WIDTH, WIDTH)], r.w_in.at[:, pl.ds(WIDTH, WIDTH)], load.at[2]),
-        pltpu.make_async_copy(
-            w_qkv.at[:, pl.ds(2 * WIDTH, WIDTH)], r.w_in.at[:, pl.ds(2 * WIDTH, WIDTH)], load.at[3]
-        ),
-        pltpu.make_async_copy(w_o, r.w_back, load.at[4]),
-    ]
+    moves = [(predictions, r.pred_in), (latent, r.lat.at[1]), (target, r.targ_in), (w_out, r.w_out_in)]
+    for j in range(3):
+        third_cols = pl.ds(j * WIDTH, WIDTH)
+        moves.append((w_qkv.at[:, third_cols], r.w_in.at[:, third_cols]))
+    moves.append((w_o, r.w_back))
+    loads = [pltpu.make_async_copy(src, dst, load.at[i]) for i, (src, dst) in enumerate(moves)]
     for copy in loads:
         copy.start()
 
@@ -182,8 +183,9 @@
 
     r.pred_p[:, 96:, :] = jnp.zeros((2, 32, 128), F32)
     channels = target.shape[0]
+    loads[0].wait()
     for m in range(MEMBERS_DEV):
-        r.pred_p[m, :channels, :] = predictions[:, m, :]
+        r.pred_p[m, :channels, :] = r.pred_in[pl.ds(m, channels, stride=MEMBERS_DEV), :]
 
     pl.semaphore_wait(barrier, len(greeted))
 
@@ -208,11 +210,13 @@
 
     r.targ_p[...] = jnp.zeros((128, 128), F32)
     r.w_dec[...] = jnp.zeros((128, WIDTH), BF16)
-    r.targ_p[:channels, :] = target[...]
-    r.w_dec[:channels, :] = w_out[...]
-    head_row = lax.broadcasted_iota(jnp.int32, (512, GROUP), 0) // 128
-    head_col = lax.broadcasted_iota(jnp.int32, (512, GROUP), 1) // 64
-    r.mask[...] = jnp.where(head_row == head_col, jnp.float32(1.0), jnp.float32(0.0)).astype(BF16)
+    loads[2].wait()
+    loads[3].wait()
+    r.targ_p[:channels, :] = r.targ_in[...]
+    r.w_dec[:channels, :] = r.w_out_in[...]
+    lane = lax.broadcasted_iota(jnp.int32, (128, 128), 1)
+    for h in range(2):
+        r.mask[h] = jnp.where(lane // 64 == h, jnp.float32(1.0), jnp.float32(0.0)).astype(BF16)
 
     every = slice(0, ROWS)
 
@@ -239,9 +243,9 @@
             else:
                 r.vx[block, rows, at] = piece
 
-    loads[0].wait()
+    loads[1].wait()
     normalise(1, True)
-    for copy in loads[1:]:
+    for copy in loads[4:]:
         copy.wait()
     project(1, 0, 6)
 
@@ -324,7 +328,13 @@
     ]
 
     def spread(block):
-        return jnp.concatenate([block, block, block, block], axis=0) * r.mask[...]
+        left, right = block[:, :128], block[:, 128:]
+        zero = jnp.zeros((128, 128), BF16)
+        return jnp.concatenate(
+            [jnp.concatenate([left * r.mask[h], zero], axis=1) for h in range(2)]
+            + [jnp.concatenate([zero, right * r.mask[h]], axis=1) for h in range(2)],
+            axis=0,
+        )
 
     def per_head(left, right):
         return jnp.concatenate(
@@ -524,7 +534,6 @@
     pair_o.wait_recv()
     pair_q.wait_recv()
     arrive0 = first(0)
-    own_terms(0)
 
     for side, copy in ((near, crh_near), (far, crh_far)):
         copy.wait_recv()
@@ -565,6 +574,7 @@
     pair_k.wait_recv()
     pair_v.wait_recv()
     arrive1 = first(1)
+    own_terms(0)
     arrive0 = second(0, arrive0)
     own_terms(1)
 
@@ -580,7 +590,9 @@
         - jnp.mean(dnorm, axis=-1, keepdims=True)
         - norm * jnp.mean(dnorm * norm, axis=-1, keepdims=True)
     )
-    g_latent[...] = (r.daf[...] + dlayer).astype(BF16)
+    r.g_stage[...] = (r.daf[...] + dlayer).astype(BF16)
+    stored = pltpu.make_async_copy(r.g_stage, g_latent, load.at[8])
+    stored.start()
 
     arrive1 = second(1, arrive1)
     own, other = finish(0, arrive0)
@@ -597,13 +609,17 @@
     place_both(g_qkv, WIDTH + 384, own[1][:, :128], other[1][:, :128])
     place_both(g_qkv, 2 * WIDTH, own[1][:, 128:], other[1][:, 128:])
     place_both(g_qkv, 2 * WIDTH + 256, own[2], other[2])
+    stored.wait()
     for copy in sent:
         copy.wait_send()
 
 
 def hand_over(*refs):
-    for source, target in zip(refs[:4], refs[4:]):
-        target[...] = source[...]
+    copies = [pltpu.make_async_copy(refs[i], refs[4 + i], refs[8].at[i]) for i in range(4)]
+    for copy in copies:
+        copy.start()
+    for copy in copies:
+        copy.wait()
 
 
 def on_device(latent, predictions, target, area_weight, slab_count, w_qkv, w_o, w_out):
@@ -622,21 +638,22 @@
     grad_latent, grad_qkv, grad_o, grad_out = pl.pallas_call(
         kernel,
         out_shape=shapes,
-        in_specs=[hbm, vmem, vmem, vmem, smem, hbm, hbm, vmem],
-        out_specs=[vmem] * 4,
+        in_specs=[hbm, hbm, hbm, vmem, smem, hbm, hbm, hbm],
+        out_specs=[hbm, vmem, vmem, vmem],
         scratch_shapes=SHAPES,
         compiler_params=pltpu.CompilerParams(
             collective_id=0, has_side_effects=True, vmem_limit_bytes=62 * 1024 * 1024
         ),
     )(
-        latent.reshape(rows, width), predictions.transpose(1, 0, 2), target, area_weight.reshape(1, points),
+        latent.reshape(rows, width), predictions.transpose(1, 0, 2).reshape(members_here * channels, points), target, area_weight.reshape(1, points),
         slab_count, w_qkv, w_o, w_out.T,
     )
     grad_latent, grad_qkv, grad_o, grad_out = pl.pallas_call(
         hand_over,
         out_shape=shapes,
-        in_specs=[vmem] * 4,
-        out_specs=[vmem] * 4,
+        in_specs=[hbm] * 4,
+        out_specs=[hbm] * 4,
+        scratch_shapes=[pltpu.SemaphoreType.DMA((4,))],
     )(grad_latent, grad_qkv, grad_o, grad_out)
     return grad_latent.reshape(latent.shape), grad_qkv, grad_o, grad_out
 

time: 71.4 us -> 89.5 us (1.25)
  Pallas kernels: 69.9 us -> 87.9 us
    pallas_call x2, Pallas kernels: 69.9 us -> 87.9 us  [the longest x1 66.8 us: on_device(): pl.pallas_call(kernel, out_shape=shapes, in_specs=[hbm, hbm, hbm, vmem, s...]
where the time goes in v4:
time: 89.5 us; the launch traced here: 89.4 us
  Pallas kernels  87.9 us (98%)
  between operations  1.47 us (2%)
    pallas_call x1, Pallas kernels, on_device(): pl.pallas_call(kernel, out_shape=shapes, in_specs=[hbm, hbm, hbm, vmem, s...  66.8 us
    pallas_call x1, Pallas kernels, on_device(): pl.pallas_call(hand_over, out_shape=shapes, in_specs=[hbm] * 4, out_specs...  21.1 us

profile of v4, /device:TPU:1, one launch (start us, length us, event | category | flops | bytes accessed | tf_op | source)
XLA Modules:
  0.0 89.4 jit_solution(6737375245492333872)
XLA Ops:
  1.3 66.8 %shard_map.111 = (bf16[256,1024]{1,0:T(8,128)(2,1)}, f32[8,3072]{1,0:T(8,128)}, f32[8,1024]{1,0:T(8,128)}, f32[8,100]{1,0:T(8,128)}) custom-call(bf16[256,1024]{1,0:T(8,128)(2,1)} %bitcast.7, f32[200,128]{1,0:T(8,128)} %bitcast.9, f32[100,128]{1,0:T(8,128)} %target.1, f32[1,128]{1,0:T(1,128)} %bitcast.10, s32[1]{0:T(128)S(6)} %copy.12.slab_count, ...), custom_call_target="tpu_custom_call" | custom-call | tf_op jit(solution)/shard_map/pallas_call | solution.py:638
  68.1 21.1 %shard_map.112 = (bf16[256,1024]{1,0:T(8,128)(2,1)}, f32[8,3072]{1,0:T(8,128)}, f32[8,1024]{1,0:T(8,128)}, f32[8,100]{1,0:T(8,128)}) custom-call(bf16[256,1024]{1,0:T(8,128)(2,1)} %get-tuple-element.12.refs_0_, f32[8,3072]{1,0:T(8,128)} %get-tuple-element.13.refs_1_, f32[8,1024]{1,0:T(8,128)} %get-tuple-element.14.refs_2_, f32[8,100]{1,0:T(8,128)} %get-tuple-element.15.refs_3_), custom_call_target="tpu_custom_call" | custom-call | tf_op jit(solution)/shard_map/pallas_call | solution.py:651

commit v5 on v4

--- a/solution.py
+++ b/solution.py
@@ -400,13 +400,6 @@
     r.d_o[:ROWS] = mine(r.daf_b.at[1], slice(0, ROWS), 0)
     r.d_q[:ROWS] = mine(r.dqkv, slice(0, ROWS), 0)
 
-    after = r.lat[1].astype(F32) + dot(r.att[...], r.w_back[...])
-    lay(after.astype(BF16), [(r.ft, ORDERS[2])], 0)
-    lay(r.att[...], ats, 0)
-    for copy in pair_a:
-        copy.wait_recv()
-    lay(r.att_o[...], ats, ROWS)
-
     def terms(wave, p, dest):
         at = pl.ds(pl.multiple_of(dest * 256, 256), 256)
         if wave == 0:
@@ -436,33 +429,30 @@
             ref[index, rows, begin:end] = value.astype(dtype)
             begin = end
 
-    def first(wave):
-        copies = {}
-
-        def go(p, slot, offset):
-            copies[p, slot] = push(
-                wave, p, slot, r.send1[wave][p].at[slot], r.recv1[wave][p].at[slot], neighbour(p, 0, offset)
-            )
-
-        for p in range(3):
-            values = terms(wave, p, place.ahead(ORDERS[p][0], 2))
-            put(r.send1[wave][p], 0, [v[:128] for v in values], BF16)
-            put(r.send1[wave][p], 1, [v[128:] for v in values], BF16)
-            go(p, 0, 1)
-            go(p, 1, 3)
-        for p in range(3):
-            values = terms(wave, p, place.ahead(ORDERS[p][0], 1))
-            put(r.send1[wave][p], 2, [v[128:] for v in values], BF16)
-            put(r.hold[wave][p], 0, [v[:128] for v in values], F32)
-            go(p, 2, 1)
-            values = terms(wave, p, place.ahead(ORDERS[p][0], 3))
-            put(r.send1[wave][p], 3, [v[:128] for v in values], BF16)
-            put(r.hold[wave][p], 1, [v[128:] for v in values], F32)
-            go(p, 3, 3)
-        return copies
-
-    def relay(wave, copies):
-        for p in range(3):
+    def go(wave, copies, p, slot, offset):
+        copies[p, slot] = push(
+            wave, p, slot, r.send1[wave][p].at[slot], r.recv1[wave][p].at[slot], neighbour(p, 0, offset)
+        )
+
+    def first_relayed(wave, copies, p):
+        values = terms(wave, p, place.ahead(ORDERS[p][0], 2))
+        put(r.send1[wave][p], 0, [v[:128] for v in values], BF16)
+        put(r.send1[wave][p], 1, [v[128:] for v in values], BF16)
+        go(wave, copies, p, 0, 1)
+        go(wave, copies, p, 1, 3)
+
+    def first_direct(wave, copies, p):
+        values = terms(wave, p, place.ahead(ORDERS[p][0], 1))
+        put(r.send1[wave][p], 2, [v[128:] for v in values], BF16)
+        put(r.hold[wave][p], 0, [v[:128] for v in values], F32)
+        go(wave, copies, p, 2, 1)
+        values = terms(wave, p, place.ahead(ORDERS[p][0], 3))
+        put(r.send1[wave][p], 3, [v[:128] for v in values], BF16)
+        put(r.hold[wave][p], 1, [v[128:] for v in values], F32)
+        go(wave, copies, p, 3, 3)
+
+    def relay(wave, copies, parts=(0, 1, 2)):
+        for p in parts:
             for half, offset in ((0, 1), (1, 3)):
                 copies[p, half].wait_recv()
                 r.send1[wave][p][4 + half] = (r.hold[wave][p][half] + r.recv1[wave][p][half].astype(F32)).astype(BF16)
@@ -531,9 +521,21 @@
         out[:, begin : begin + width] = jnp.where(core == 0, own, other)
         out[:, begin + HALF : begin + HALF + width] = jnp.where(core == 0, other, own)
 
+    arrive0 = {}
+    pair_q.wait_recv()
+    first_relayed(0, arrive0, 0)
+    first_direct(0, arrive0, 0)
+    lay(r.att[...], ats, 0)
     pair_o.wait_recv()
-    pair_q.wait_recv()
-    arrive0 = first(0)
+    for copy in pair_a:
+        copy.wait_recv()
+    lay(r.att_o[...], ats, ROWS)
+    first_relayed(0, arrive0, 1)
+    after = r.lat[1].astype(F32) + dot(r.att[...], r.w_back[...])
+    lay(after.astype(BF16), [(r.ft, ORDERS[2])], 0)
+    first_relayed(0, arrive0, 2)
+    first_direct(0, arrive0, 1)
+    first_direct(0, arrive0, 2)
 
     for side, copy in ((near, crh_near), (far, crh_far)):
         copy.wait_recv()
@@ -541,8 +543,8 @@
         attend_back(side)
     project(far, 0, 2)
 
-    def other_queries(half):
-        for m in range(2):
+    def other_queries(half, members=(0, 1)):
+        for m in members:
             rows = member_rows[m]
             for u in range(2):
                 cols = group_cols(half, u)
@@ -564,16 +566,23 @@
 
     for copy in sth:
         copy.wait_recv()
-    other_queries(1 - core)
+    relay(0, arrive0, (0,))
+    other_queries(1 - core, (0,))
+    relay(0, arrive0, (1,))
+    other_queries(1 - core, (1,))
     pair_k = give(4, r.dqkv.at[:, pl.ds(pl.multiple_of(WIDTH + theirs, HALF), HALF)], r.d_k.at[high_rows])
     pair_v = give(5, r.dqkv.at[:, pl.ds(pl.multiple_of(2 * WIDTH + theirs, HALF), HALF)], r.d_v.at[high_rows])
-    relay(0, arrive0)
+    relay(0, arrive0, (2,))
     other_queries(core)
     r.d_k[:ROWS] = mine(r.dqkv, slice(0, ROWS), WIDTH)
     r.d_v[:ROWS] = mine(r.dqkv, slice(0, ROWS), 2 * WIDTH)
     pair_k.wait_recv()
     pair_v.wait_recv()
-    arrive1 = first(1)
+    arrive1 = {}
+    for p in range(3):
+        first_relayed(1, arrive1, p)
+    for p in range(3):
+        first_direct(1, arrive1, p)
     own_terms(0)
     arrive0 = second(0, arrive0)
     own_terms(1)
@@ -615,11 +624,8 @@
 
 
 def hand_over(*refs):
-    copies = [pltpu.make_async_copy(refs[i], refs[4 + i], refs[8].at[i]) for i in range(4)]
-    for copy in copies:
-        copy.start()
-    for copy in copies:
-        copy.wait()
+    for source, target in zip(refs[:4], refs[4:]):
+        target[...] = source[...]
 
 
 def on_device(latent, predictions, target, area_weight, slab_count, w_qkv, w_o, w_out):
@@ -651,9 +657,8 @@
     grad_latent, grad_qkv, grad_o, grad_out = pl.pallas_call(
         hand_over,
         out_shape=shapes,
-        in_specs=[hbm] * 4,
-        out_specs=[hbm] * 4,
-        scratch_shapes=[pltpu.SemaphoreType.DMA((4,))],
+        in_specs=[vmem] * 4,
+        out_specs=[vmem] * 4,
     )(grad_latent, grad_qkv, grad_o, grad_out)
     return grad_latent.reshape(latent.shape), grad_qkv, grad_o, grad_out
 

time: 89.5 us -> 70.2 us (0.78)
  Pallas kernels: 87.9 us -> 68.7 us
    pallas_call x1, Pallas kernels: 21.1 us -> 1.94 us  [on_device(): pl.pallas_call(hand_over, out_shape=shapes, in_specs=[vmem] * 4, out_spec...]
where the time goes in v5:
time: 70.2 us; the launch traced here: 70 us
  Pallas kernels  68.7 us (98%)
  between operations  1.29 us (2%)
    pallas_call x1, Pallas kernels, on_device(): pl.pallas_call(kernel, out_shape=shapes, in_specs=[hbm, hbm, hbm, vmem, s...  66.8 us
    pallas_call x1, Pallas kernels, on_device(): pl.pallas_call(hand_over, out_shape=shapes, in_specs=[vmem] * 4, out_spec...  1.94 us

profile of v5, /device:TPU:1, one launch (start us, length us, event | category | flops | bytes accessed | tf_op | source)
XLA Modules:
  0.0 70.0 jit_solution(10064900461094052471)
XLA Ops:
  1.3 66.8 %shard_map.111 = (bf16[256,1024]{1,0:T(8,128)(2,1)}, f32[8,3072]{1,0:T(8,128)}, f32[8,1024]{1,0:T(8,128)}, f32[8,100]{1,0:T(8,128)}) custom-call(bf16[256,1024]{1,0:T(8,128)(2,1)} %bitcast.7, f32[200,128]{1,0:T(8,128)} %bitcast.9, f32[100,128]{1,0:T(8,128)} %target.1, f32[1,128]{1,0:T(1,128)} %bitcast.10, s32[1]{0:T(128)S(6)} %copy.12.slab_count, ...), custom_call_target="tpu_custom_call" | custom-call | tf_op jit(solution)/shard_map/pallas_call | solution.py:644
  68.1 1.9 %shard_map.112 = (bf16[256,1024]{1,0:T(8,128)(2,1)}, f32[8,3072]{1,0:T(8,128)}, f32[8,1024]{1,0:T(8,128)}, f32[8,100]{1,0:T(8,128)}) custom-call(bf16[256,1024]{1,0:T(8,128)(2,1)} %get-tuple-element.12.refs_0_, f32[8,3072]{1,0:T(8,128)} %get-tuple-element.13.refs_1_, f32[8,1024]{1,0:T(8,128)} %get-tuple-element.14.refs_2_, f32[8,100]{1,0:T(8,128)} %get-tuple-element.15.refs_3_), custom_call_target="tpu_custom_call" | custom-call | tf_op jit(solution)/shard_map/pallas_call | solution.py:657

commit v6 on v5

--- a/solution.py
+++ b/solution.py
@@ -346,28 +346,31 @@
 
     def own_queries(m, half):
         rows = member_rows[m]
+        chains = []
         for u in range(2):
             cols = group_cols(half, u)
             keys = jnp.concatenate([r.kx[b, rows, cols] for b in range(3)], axis=0)
             values = jnp.concatenate([r.vx[b, rows, cols] for b in range(3)], axis=0)
             q_b = spread(r.qx[1, rows, cols])
             d_b = spread(r.dx[1, rows, cols])
-            scores = dot_nt(keys, q_b)
+            chains.append((cols, keys, values, q_b, d_b, dot_nt(keys, q_b), dot_nt(values, d_b)))
+        probs = []
+        for u, (cols, keys, values, q_b, d_b, scores, dprob) in enumerate(chains):
             scores = jnp.concatenate([scores[:128] + edge[0], scores[128:256], scores[256:] + edge[1]], axis=0)
             top = jnp.max(scores, axis=0, keepdims=True) * LOG2E
             e = jnp.exp2(scores * LOG2E - top)
             total = jnp.sum(e, axis=0, keepdims=True)
             prob = e * (1.0 / total)
-            prob_b = prob.astype(BF16)
-            dprob = dot_nt(values, d_b)
             delta = jnp.sum(dprob * prob, axis=0, keepdims=True)
             dscore = (prob * (dprob - delta)).astype(BF16)
+            probs.append((prob.astype(BF16), dscore))
+            r.stat[m, half, 2 * u : 2 * u + 1, :] = top + jnp.log2(total)
+            r.stat[m, half, 2 * u + 1 : 2 * u + 2, :] = delta
+        for (cols, keys, values, q_b, d_b, _, _), (prob_b, dscore) in zip(chains, probs):
             r.att[rows, cols] = per_head(values.T, prob_b).astype(BF16)
             r.dqkv[rows, cols] = (per_head(keys.T, dscore) * 0.125).astype(BF16)
             r.dk_acc[rows, cols] = dot(dscore[128:256], q_b)
             r.dv_acc[rows, cols] = dot(prob_b[128:256], d_b)
-            r.stat[m, half, 2 * u : 2 * u + 1, :] = top + jnp.log2(total)
-            r.stat[m, half, 2 * u + 1 : 2 * u + 2, :] = delta
 
     def send_stat(m):
         return [

time: 70.2 us -> 69.6 us (level)
  no operation moved by 1% of the time
where the time goes in v6:
time: 69.6 us; the launch traced here: 69.4 us
  Pallas kernels  68.2 us (98%)
  between operations  1.29 us (2%)
    pallas_call x1, Pallas kernels, on_device(): pl.pallas_call(kernel, out_shape=shapes, in_specs=[hbm, hbm, hbm, vmem, s...  66.2 us
    pallas_call x1, Pallas kernels, on_device(): pl.pallas_call(hand_over, out_shape=shapes, in_specs=[vmem] * 4, out_spec...  1.94 us

profile of v6, /device:TPU:1, one launch (start us, length us, event | category | flops | bytes accessed | tf_op | source)
XLA Modules:
  0.0 69.4 jit_solution(17694381072941552037)
XLA Ops:
  1.3 66.2 %shard_map.111 = (bf16[256,1024]{1,0:T(8,128)(2,1)}, f32[8,3072]{1,0:T(8,128)}, f32[8,1024]{1,0:T(8,128)}, f32[8,100]{1,0:T(8,128)}) custom-call(bf16[256,1024]{1,0:T(8,128)(2,1)} %bitcast.7, f32[200,128]{1,0:T(8,128)} %bitcast.9, f32[100,128]{1,0:T(8,128)} %target.1, f32[1,128]{1,0:T(1,128)} %bitcast.10, s32[1]{0:T(128)S(6)} %copy.12.slab_count, ...), custom_call_target="tpu_custom_call" | custom-call | tf_op jit(solution)/shard_map/pallas_call | solution.py:647
  67.5 1.9 %shard_map.112 = (bf16[256,1024]{1,0:T(8,128)(2,1)}, f32[8,3072]{1,0:T(8,128)}, f32[8,1024]{1,0:T(8,128)}, f32[8,100]{1,0:T(8,128)}) custom-call(bf16[256,1024]{1,0:T(8,128)(2,1)} %get-tuple-element.12.refs_0_, f32[8,3072]{1,0:T(8,128)} %get-tuple-element.13.refs_1_, f32[8,1024]{1,0:T(8,128)} %get-tuple-element.14.refs_2_, f32[8,100]{1,0:T(8,128)} %get-tuple-element.15.refs_3_), custom_call_target="tpu_custom_call" | custom-call | tf_op jit(solution)/shard_map/pallas_call | solution.py:660
